TPU v7x, 256 devices: a whole 4x4x8 slice. The times are simulated.
256 devices in a mesh: job: 32 (over x, y, core), seq: 8 (over z).
Axes of the slice: x: 4, y: 4, z: 8, core: 2. Of those that a mesh axis runs over, the one named last changes fastest.
Arguments:
- text_cache: bfloat16 [32, 2, 512, 4096], P('job', None, 'seq'), may hold values from -6 to 6
- source: int32 [32], replicated, may hold values from 0 to 63, as said below
- text_len: int32 [32], replicated, may hold values from 1 to 512, as said below
- query: bfloat16 [32, 2048, 3072], P('job', 'seq'), may hold values from -64 to 64
- w_text: bfloat16 [4096, 5120], P('job', 'seq'), may hold values from -0.09375 to 0.09375
- b_text: bfloat16 [5120], P('seq'), may hold values from -3 to 3
- w_key: bfloat16 [5120, 3072], P('job', 'seq'), may hold values from -0.078125 to 0.078125
- w_value: bfloat16 [5120, 3072], P('job', 'seq'), may hold values from -0.078125 to 0.078125
- b_value: bfloat16 [3072], P('seq'), may hold values from -3 to 3
Outputs:
- attended: bfloat16 [32, 2048, 3072], P('job', 'seq')
Inputs may be any that keep to these rules, and one draw needn't show every extreme that they name: `source`: entries are distinct flat cache indices; 0 and 63 occur in every draw. `text_len`: some group has 512 live text tokens and some has 1.
All inputs are finite; a program needn't handle non-finite values.
Results may differ from a plain program's by a relative error of at most 0.008.
Values may be sent and summed in bfloat16 or wider, within the bound.
A program may use at most 128 MiB of HBM per device.

v0:
```python
import jax
import jax.numpy as jnp
from jax import lax
from jax.sharding import PartitionSpec as P

HD = 128


def attend(queries, keys, values, key_live):
    score_scale = HD ** (-0.5)
    scores = (
        jnp.einsum("rhd,khd->hrk", queries, keys, preferred_element_type=jnp.float32) * score_scale
    )
    scores = jnp.where(key_live[None, None, :], scores, jnp.float32(-1e30))
    row_peak = jnp.max(scores, axis=-1, keepdims=True)
    exponent = jnp.exp(scores - row_peak)
    probabilities = (exponent / jnp.sum(exponent, axis=-1, keepdims=True)).astype(jnp.bfloat16)
    mixed = jnp.einsum("hrk,khd->rhd", probabilities, values, preferred_element_type=jnp.float32)
    return mixed.astype(jnp.bfloat16).reshape(queries.shape[0], -1)


def add_product(left, portion):
    return jnp.dot(left, portion, preferred_element_type=jnp.float32)


def body(text_cache, source, text_len, query, w_text, b_text, w_key, w_value, b_value):
    groups = lax.axis_size("job")
    group_index = lax.axis_index("job")
    cached = text_cache[0]
    slot_count, rows_local, text_width = cached.shape
    portion_rows = rows_local // groups
    spread = lax.all_to_all(
        cached.reshape(slot_count, groups, portion_rows, text_width),
        "job",
        split_axis=1,
        concat_axis=1,
        tiled=True,
    )
    holder = source // slot_count
    slot_of = source % slot_count
    picked = spread[slot_of, holder]
    arrived = lax.all_to_all(picked, "job", split_axis=0, concat_axis=0, tiled=True).reshape(
        rows_local, text_width
    )
    text_rows = lax.all_gather(arrived, "seq", axis=0, tiled=True)
    text_count = text_rows.shape[0]
    preact = add_product(text_rows, lax.all_gather(w_text, "job", axis=0, tiled=True))
    hidden_part = jax.nn.gelu(preact + b_text.astype(jnp.float32), approximate=True).astype(
        jnp.bfloat16
    )
    hidden = lax.all_gather(hidden_part, "seq", axis=1, tiled=True)

    def single_step(portion):
        return add_product(hidden, portion)

    key_sums = single_step(lax.all_gather(w_key, "job", axis=0, tiled=True))
    value_sums = single_step(lax.all_gather(w_value, "job", axis=0, tiled=True))
    keys = key_sums.astype(jnp.bfloat16)
    values = (value_sums + b_value.astype(jnp.float32)).astype(jnp.bfloat16)
    key_live = jnp.arange(text_count) < text_len[group_index]
    queries = query[0]
    video_local = queries.shape[0]
    all_keys, all_values = (
        lax.all_gather(keys, "seq", axis=1, tiled=True),
        lax.all_gather(values, "seq", axis=1, tiled=True),
    )
    result = attend(
        queries.reshape(video_local, -1, HD),
        all_keys.reshape(text_count, -1, HD),
        all_values.reshape(text_count, -1, HD),
        key_live,
    )
    return result[None]


def solution(mesh):
    in_specs = (
        P("job", None, "seq", None),
        P(),
        P(),
        P("job", "seq", None),
        P("job", "seq"),
        P("seq"),
        P("job", "seq"),
        P("job", "seq"),
        P("seq"),
    )
    out_specs = P("job", "seq", None)
    return jax.shard_map(body, mesh=mesh, in_specs=in_specs, out_specs=out_specs, check_vma=False)
```

profile of v0, /device:TPU:1, one launch (start us, length us, event | category | flops | bytes accessed | tf_op | source)
XLA Modules:
  0.0 442.9 jit_solution(1020585032217924011)
XLA Ops:
  6.5 0.0 copy-start.3
  6.5 2.3 copy.20
  8.9 0.0 copy-start.1
  8.9 2.1 copy.21
  10.9 8.6 %all-to-all-start = ((bf16[2,32,2,4096]{3,2,0,1:T(2,128)(2,1)}), bf16[2,32,2,4096]{3,2,0,1:T(2,128)(2,1)S(1)}, u32[]{:S(2)}, u32[]{:S(2)}) async-start(bf16[2,32,2,4096]{3,2,0,1:T(2,128)(2,1)} %copy.21), calls=%async_computation | async-start | bytes 2097152 | tf_op jit(solution)/shard_map/all_to_all | solution.py:32
  19.5 0.0 all-gather.8.cloned.1.call-start
  19.6 0.0 copy-done.3
  19.6 16.8 %all-to-all-done = bf16[2,32,2,4096]{3,2,0,1:T(2,128)(2,1)S(1)} async-done(((bf16[2,32,2,4096]{3,2,0,1:T(2,128)(2,1)}), bf16[2,32,2,4096]{3,2,0,1:T(2,128)(2,1)S(1)}, u32[]{:S(2)}, u32[]{:S(2)}) %all-to-all-start) | async-done | bytes 1048608 | tf_op jit(solution)/shard_map/all_to_all | solution.py:32
  36.5 1.6 gather_fusion
  38.1 15.4 %all_to_all.10 = bf16[32,2,4096]{2,1,0:T(2,128)(2,1)S(1)} all-to-all(bf16[32,2,4096]{2,1,0:T(2,128)(2,1)S(1)} %gather_fusion), channel_id=1, replica_groups=mesh['job'=32,'seq'=8] {'job'}, dimensions={0} | all-to-all | bytes 1048576 | tf_op jit(solution)/shard_map/all_to_all | solution.py:42
  53.5 1.0 reshape.17
  54.4 0.0 all-gather.8.cloned.1.call-update
  54.5 0.0 all-gather.10.cloned.1.call-start
  54.5 0.7 all-gather.10.cloned.1.call-update
  55.2 0.0 all-gather.18.cloned.1.call-start
  55.3 0.7 all-gather.18.cloned.1.call-update
  56.0 0.0 all-gather.12.cloned.1.call-start
  56.0 0.0 copy-done.1
  56.0 52.3 %all-gather.8.cloned.1.call-done = bf16[512,4096]{1,0:T(8,128)(2,1)} async-done(((bf16[64,4096]{1,0:T(8,128)(2,1)}), bf16[512,4096]{1,0:T(8,128)(2,1)}) %all-gather.8.cloned.1.call-update) | async-done | bytes 4194320 | tf_op jit(solution)/shard_map/all_gather | solution.py:45
  108.3 54.1 %all-gather.10.cloned.1.call-done = bf16[4096,640]{1,0:T(8,128)(2,1)} async-done(((bf16[128,640]{1,0:T(8,128)(2,1)}), bf16[4096,640]{1,0:T(8,128)(2,1)}) %all-gather.10.cloned.1.call-update) | async-done | bytes 5242896 | tf_op jit(solution)/shard_map/all_gather | solution.py:47
  162.4 8.2 %fusion.21 = bf16[512,640]{1,0:T(8,128)(2,1)} fusion(bf16[512,4096]{1,0:T(8,128)(2,1)} %all-gather.8.cloned.1.call-done, bf16[4096,640]{1,0:T(8,128)(2,1)} %all-gather.10.cloned.1.call-done, f32[640]{0:T(1024)S(1)} %convert_element_type.24), kind=kOutput, calls=%fused_computation.26 | convolution fusion | flops 2687631360 | bytes 10095104 | tf_op jit(solution)/shard_map/dot_general | solution.py:23
  170.6 0.0 all-gather.12.cloned.1.call-update
  170.6 0.0 all-gather.14.cloned.1.call-start
  170.6 0.5 all-gather.14.cloned.1.call-update
  171.2 0.0 copy-start.2
  171.2 0.0 all-gather.20.cloned.1.call-start
  171.2 43.9 %all-gather.18.cloned.1.call-done = bf16[5120,384]{1,0:T(8,128)(2,1)} async-done(((bf16[160,384]{1,0:T(8,128)(2,1)}), bf16[5120,384]{1,0:T(8,128)(2,1)}) %all-gather.18.cloned.1.call-update) | async-done | bytes 3932176 | tf_op jit(solution)/shard_map/all_gather | solution.py:56
  215.1 65.4 %all-gather.12.cloned.1.call-done = bf16[512,5120]{1,0:T(8,128)(2,1)} async-done(((bf16[512,640]{1,0:T(8,128)(2,1)}), bf16[512,5120]{1,0:T(8,128)(2,1)}) %all-gather.12.cloned.1.call-update) | async-done | bytes 5242896 | tf_op jit(solution)/shard_map/all_gather | solution.py:51
  280.5 7.3 %convolution_convert_fusion = bf16[512,384]{1,0:T(8,128)(2,1)} fusion(bf16[512,5120]{1,0:T(8,128)(2,1)} %all-gather.12.cloned.1.call-done, bf16[5120,384]{1,0:T(8,128)(2,1)} %all-gather.18.cloned.1.call-done), kind=kOutput, calls=%fused_computation.29 | convolution fusion | flops 2013462528 | bytes 9568256 | tf_op jit(solution)/shard_map/dot_general | solution.py:23
  287.8 0.0 all-gather.20.cloned.1.call-update
  287.8 0.2 all-gather.16.cloned.1.call-start
  288.0 0.0 copy-done.2
  288.1 0.0 copy-start
  288.1 0.0 copy-start.4
  288.1 44.6 %all-gather.14.cloned.1.call-done = bf16[5120,384]{1,0:T(8,128)(2,1)} async-done(((bf16[160,384]{1,0:T(8,128)(2,1)}), bf16[5120,384]{1,0:T(8,128)(2,1)}) %all-gather.14.cloned.1.call-update) | async-done | bytes 3932176 | tf_op jit(solution)/shard_map/all_gather | solution.py:57
  332.7 7.3 %fusion.22 = bf16[512,384]{1,0:T(8,128)(2,1)} fusion(bf16[512,5120]{1,0:T(8,128)(2,1)} %all-gather.12.cloned.1.call-done, bf16[5120,384]{1,0:T(8,128)(2,1)} %all-gather.14.cloned.1.call-done, f32[384]{0:T(512)S(1)} %convert_element_type.26), kind=kOutput, calls=%fused_computation.28 | convolution fusion | flops 2013659136 | bytes 9569792 | tf_op jit(solution)/shard_map/dot_general | solution.py:23
  340.0 0.0 all-gather.16.cloned.1.call-update
  340.0 0.0 copy-done
  340.0 0.3 copy.30
  340.4 0.0 copy-done.4
  340.4 0.6 dynamic_slice.3
  341.0 0.6 iota_compare_fusion
  341.6 35.9 %all-gather.20.cloned.1.call-done = bf16[512,3072]{1,0:T(8,128)(2,1)} async-done(((bf16[512,384]{1,0:T(8,128)(2,1)}), bf16[512,3072]{1,0:T(8,128)(2,1)}) %all-gather.20.cloned.1.call-update) | async-done | bytes 3145744 | tf_op jit(solution)/shard_map/all_gather | solution.py:64
  377.5 3.7 fusion.9
  381.2 9.1 %fusion.30 = (f32[24,256]{1,0:T(8,128)S(1)}, f32[24,256,512]{1,2,0:T(8,128)}) fusion(f32[24,512,256]{2,1,0:T(8,128)S(1)} %fusion.9, pred[512]{0:T(512)(128)(4,1)S(1)} %iota_compare_fusion), kind=kOutput, calls=%fused_computation.45 | output fusion | flops 18874880 | bytes 25190912 | tf_op jit(solution)/shard_map/sub | solution.py:16
  390.3 33.1 %all-gather.16.cloned.1.call-done = bf16[512,3072]{1,0:T(8,128)(2,1)} async-done(((bf16[512,384]{1,0:T(8,128)(2,1)}), bf16[512,3072]{1,0:T(8,128)(2,1)}) %all-gather.16.cloned.1.call-update) | async-done | bytes 3145744 | tf_op jit(solution)/shard_map/all_gather | solution.py:65
  423.4 3.2 copy.28
  426.6 6.8 %fusion.12 = bf16[24,128,256]{2,1,0:T(8,128)(2,1)} fusion(bf16[512,24,128]{0,2,1:T(8,128)(2,1)S(1)} %bitcast.36, f32[24,256,512]{1,2,0:T(8,128)} %get-tuple-element.6, f32[24,256]{1,0:T(8,128)S(1)} %get-tuple-element.5), kind=kOutput, calls=%fused_computation.16 | convolution fusion | flops 812384256 | bytes 17326080 | tf_op jit(solution)/shard_map/hrk,khd->rhd/dot_general | solution.py:18
  433.4 2.6 copy.26
  (3 shorter events, 0.0 us)
Async XLA Ops:
  6.5 13.1 %copy-start.3 = (s32[32]{0:T(128)S(1)}, s32[32]{0:T(128)}, u32[]{:S(2)}) copy-start(s32[32]{0:T(128)} %param.10) | copy-start | bytes 388
  8.9 47.1 %copy-start.1 = (bf16[640]{0:T(1024)(128)(2,1)S(1)}, bf16[640]{0:T(1024)(128)(2,1)}, u32[]{:S(2)}) copy-start(bf16[640]{0:T(1024)(128)(2,1)} %param.14) | copy-start | bytes 3844
  10.9 25.5 %all-to-all-start = ((bf16[2,32,2,4096]{3,2,0,1:T(2,128)(2,1)}), bf16[2,32,2,4096]{3,2,0,1:T(2,128)(2,1)S(1)}, u32[]{:S(2)}, u32[]{:S(2)}) async-start(bf16[2,32,2,4096]{3,2,0,1:T(2,128)(2,1)} %copy.21), calls=%async_computation | async-start | bytes 2097152 | tf_op jit(solution)/shard_map/all_to_all | solution.py:32
  19.5 88.7 %all-gather.8.cloned.1.call-start = ((), (), s32[]{:S(2)}) async-start(), calls=%async_computation.2 | async-start | bytes 4718592 | tf_op jit(solution)/shard_map/all_gather | solution.py:45
  54.5 107.9 %all-gather.10.cloned.1.call-start = ((), (), s32[]{:S(2)}) async-start(), calls=%async_computation.3 | async-start | bytes 5406720 | tf_op jit(solution)/shard_map/all_gather | solution.py:47
  55.2 159.9 %all-gather.18.cloned.1.call-start = ((), (), s32[]{:S(2)}) async-start(), calls=%async_computation.7 | async-start | bytes 4055040 | tf_op jit(solution)/shard_map/all_gather | solution.py:56
  56.0 224.5 %all-gather.12.cloned.1.call-start = ((), (), s32[]{:S(2)}) async-start(), calls=%async_computation.4 | async-start | bytes 5898240 | tf_op jit(solution)/shard_map/all_gather | solution.py:51
  170.6 162.1 %all-gather.14.cloned.1.call-start = ((), (), s32[]{:S(2)}) async-start(), calls=%async_computation.5 | async-start | bytes 4055040 | tf_op jit(solution)/shard_map/all_gather | solution.py:57
  171.2 116.8 %copy-start.2 = (bf16[384]{0:T(512)(128)(2,1)S(1)}, bf16[384]{0:T(512)(128)(2,1)}, u32[]{:S(2)}) copy-start(bf16[384]{0:T(512)(128)(2,1)} %param.17) | copy-start | bytes 2308
  171.2 206.3 %all-gather.20.cloned.1.call-start = ((), (), s32[]{:S(2)}) async-start(), calls=%async_computation.8 | async-start | bytes 3538944 | tf_op jit(solution)/shard_map/all_gather | solution.py:64
  287.8 135.6 %all-gather.16.cloned.1.call-start = ((), (), s32[]{:S(2)}) async-start(), calls=%async_computation.6 | async-start | bytes 3538944 | tf_op jit(solution)/shard_map/all_gather | solution.py:65
  288.1 52.0 %copy-start = (bf16[1,256,3072]{2,1,0:T(8,128)(2,1)S(1)}, bf16[1,256,3072]{2,1,0:T(8,128)(2,1)}, u32[]{:S(2)}) copy-start(bf16[1,256,3072]{2,1,0:T(8,128)(2,1)} %param.12) | copy-start | bytes 4718596
  288.1 52.3 %copy-start.4 = (s32[32]{0:T(128)S(1)}, s32[32]{0:T(128)}, u32[]{:S(2)}) copy-start(s32[32]{0:T(128)} %param.11) | copy-start | bytes 388
Sparse Core Ops, SparseCore 0:
  54.6 53.6 all-gather.7
  110.8 51.4 all-gather.9
  164.9 50.1 all-gather.17
  216.8 63.6 all-gather.11
  282.9 49.7 all-gather.13
  334.3 43.1 all-gather.19
  379.3 44.0 all-gather.15
where the time goes:
time: 444 us; the launch traced here: 443 us
  waiting for transfers between devices  348 us (78%)
  matrix products  33.4 us (8%)
  blocking collectives  15.4 us (3%)
  local copies, waits for them, and re-layouts  13.7 us (3%)
  between operations  13.6 us (3%)
  other arithmetic  9.71 us (2%)
  starting transfers between devices  9.05 us (2%)
    all_gather x1, waiting for transfers between devices, body(): hidden = lax.all_gather(hidden_part, 'seq', axis=1, tiled=True)  65.4 us
    all_gather x1, waiting for transfers between devices, body(): lax.all_gather(w_text, 'job', axis=0, tiled=True)  54.1 us
    all_gather x1, waiting for transfers between devices, body(): text_rows = lax.all_gather(arrived, 'seq', axis=0, tiled=True)  52.3 us
    all_gather x1, waiting for transfers between devices, body(): value_sums = single_step(lax.all_gather(w_value, 'job', axis=0, tiled=True))  44.6 us
    all_gather x1, waiting for transfers between devices, body(): key_sums = single_step(lax.all_gather(w_key, 'job', axis=0, tiled=True))  43.9 us
    all_gather x1, waiting for transfers between devices, body(): lax.all_gather(keys, 'seq', axis=1, tiled=True)  35.9 us
    all_gather x1, waiting for transfers between devices, body(): lax.all_gather(values, 'seq', axis=1, tiled=True)  33.1 us
    dot_general x3, matrix products, add_product(): return jnp.dot(left, portion, preferred_element_type=jnp.float32)  22.9 us
  transfers between devices with their start and end apart: 8, of which 8 were waited for; matrix products, arithmetic and copies ran while one was open for 8% of the time, Pallas kernels for 0%

commit v1 on v0

v1 whole, which is shorter than its diff:
```python
import functools

import jax
import jax.numpy as jnp
from jax import lax
from jax.experimental import pallas as pl
from jax.experimental.pallas import tpu as pltpu
from jax.sharding import PartitionSpec as P

MESH = pl.DeviceIdType.MESH
HD = 128
NJ, NZ, NX = 32, 8, 4
TXT, DT, DM, HQ, VR = 512, 4096, 5120, 3072, 256
ROWS = TXT // NZ
HB, KB = DM // NZ, HQ // NZ
WIN = 256
DEPTHS = (DT // NJ, DM // NJ, DM // NJ)
N_SEND = 224


def kernel(
    cache, source, text_len, query, w_text, w_key, w_value, bias, out_hbm,
    slabs, picked, txt, wt, wk, wv, hid, kall, vall, prob, qv, ov, bias_far, acc,
    send_sem, route_send, route_recv, local_sem, start_recv, flow_recv, twin_recv,
    text_recv, hid_recv, key_recv, value_recv, bias_recv, query_sem,
):
    me, z = lax.axis_index("job"), lax.axis_index("seq")
    core, chip = lax.rem(me, 2), me // 2
    x, y = chip // NX, lax.rem(chip, NX)
    u, v = jnp.where(core == 0, x, y), jnp.where(core == 0, y, x)
    step_u, step_v = 8 - 6 * core, 2 + 6 * core
    up, down, far = lax.rem(z + 1, NZ), lax.rem(z + NZ - 1, NZ), lax.rem(z + 4, NZ)
    twin = me + 1 - 2 * core

    def block(h):
        return z if h == 0 else far

    def at_uv(a, b):
        return lax.rem(u + a + NX, NX) * step_u + lax.rem(v + b + NX, NX) * step_v

    pending = []

    def send(src, dst, recv, job, seq):
        n = len(pending)
        copy = pltpu.make_async_remote_copy(
            src_ref=src, dst_ref=dst, send_sem=send_sem.at[n], recv_sem=recv,
            device_id={"job": job, "seq": seq}, device_id_type=MESH,
        )
        copy.start()
        pending.append(copy)

    def arrive(ref, sem):
        pltpu.make_async_copy(ref, ref, sem).wait()

    barrier = pltpu.get_barrier_semaphore()

    def greet(job, seq):
        pl.semaphore_signal(barrier, inc=1, device_id={"job": job, "seq": seq}, device_id_type=MESH)

    @pl.loop(1, NJ)
    def _(i):
        greet(lax.rem(me + i, NJ), z)

    greet(me, up)
    greet(me, down)
    greet(me, far)
    greet(twin, far)
    pl.semaphore_wait(barrier, NJ - 1 + 4)

    def slab_copy(i):
        to = lax.rem(me + i, NJ)
        return pltpu.make_async_remote_copy(
            src_ref=cache.at[0, :, :, pl.ds(pl.multiple_of(to * 128, 128), 128)],
            dst_ref=slabs.at[pl.ds(2 * me, 2)],
            send_sem=route_send.at[0, i], recv_sem=route_recv.at[0],
            device_id={"job": to, "seq": z}, device_id_type=MESH,
        )

    @pl.loop(1, NJ)
    def _(i):
        slab_copy(i).start()

    my_columns = pl.ds(pl.multiple_of(me * 128, 128), 128)
    own_slab = pltpu.make_async_copy(
        cache.at[0, :, :, my_columns], slabs.at[pl.ds(2 * me, 2)], local_sem.at[0]
    )
    own_slab.start()

    weights = ((w_text, wt), (w_key, wk), (w_value, wv))
    first = []
    for t, (shard, whole) in enumerate(weights):
        n = DEPTHS[t]
        rows = pl.ds(pl.multiple_of(me * n, 32), n)
        keep = pltpu.make_async_copy(shard, whole.at[0, rows], start_recv.at[t, 0])
        give = pltpu.make_async_remote_copy(
            src_ref=shard, dst_ref=whole.at[0, rows], send_sem=local_sem.at[1 + t],
            recv_sem=start_recv.at[t, 1], device_id={"job": twin, "seq": z}, device_id_type=MESH,
        )
        pl.when(core == 0)(keep.start)
        pl.when(core == 1)(give.start)
        first.append(give)
        send(shard, whole.at[1, rows], start_recv.at[t, core], chip * 2 + 1, far)
    send(bias, bias_far, bias_recv.at[0], me, far)
    fetch = [
        pltpu.make_async_copy(query.at[0, :, pl.ds(b * KB, KB)], qv.at[b], query_sem.at[b])
        for b in range(NZ)
    ]
    for copy in fetch:
        copy.start()

    def piece(t, a, b, part=None):
        n = 2 * DEPTHS[t]
        base = (lax.rem(u + a + NX, NX) * (step_u // 2) + lax.rem(v + b + NX, NX) * (step_v // 2)) * n
        if part is None:
            return weights[t][1].at[core, pl.ds(pl.multiple_of(base, 32), n)]
        base = base + part * (n // 2)
        return weights[t][1].at[core, pl.ds(pl.multiple_of(base, 32), n // 2)]

    def give(t, a, b, da, db, slot, part=None):
        ref = piece(t, a, b, part)
        send(ref, ref, flow_recv.at[t, slot], at_uv(da, db) + core, z)

    def share(t, a, b):
        ref = piece(t, a, b)
        send(ref, ref, twin_recv.at[t], twin, z)

    def across(t, a, index):
        give(t, a, 0, 0, 1, 4 + 4 * index)
        give(t, a, 0, 0, -1, 5 + 4 * index)
        share(t, a, 0)

    def flow_own(t):
        arrive(weights[t][0], start_recv.at[t, 0])
        arrive(weights[t][0], start_recv.at[t, 1])
        give(t, 0, 0, 1, 0, 0)
        give(t, 0, 0, -1, 0, 1)
        across(t, 0, 0)

    def flow_near(t):
        arrive(piece(t, -1, 0), flow_recv.at[t, 0])
        give(t, -1, 0, 1, 0, 2, 0)
        across(t, -1, 1)
        arrive(piece(t, 1, 0), flow_recv.at[t, 1])
        give(t, 1, 0, -1, 0, 3, 1)
        across(t, 1, 2)

    def flow_far(t):
        arrive(piece(t, 2, 0, 0), flow_recv.at[t, 2])
        arrive(piece(t, 2, 0, 1), flow_recv.at[t, 3])
        across(t, 2, 3)

    PLACES = (0, -1, 1, 2)

    def flow_second(t, index):
        a = PLACES[index]
        arrive(piece(t, a, -1), flow_recv.at[t, 4 + 4 * index])
        give(t, a, -1, 0, 1, 6 + 4 * index, 0)
        share(t, a, -1)
        arrive(piece(t, a, 1), flow_recv.at[t, 5 + 4 * index])
        give(t, a, 1, 0, -1, 7 + 4 * index, 1)
        share(t, a, 1)

    def flow_last(t, index):
        a = PLACES[index]
        arrive(piece(t, a, 2, 0), flow_recv.at[t, 6 + 4 * index])
        arrive(piece(t, a, 2, 1), flow_recv.at[t, 7 + 4 * index])
        share(t, a, 2)

    def flow_twin(t):
        arrive(weights[t][1].at[1 - core], twin_recv.at[t])

    flow_own(0)

    own_slab.wait()
    arrive(slabs.at[pl.ds(0, 2 * (NJ - 1))], route_recv.at[0])

    @pl.loop(0, NJ)
    def _(g):
        picked[g] = slabs[source[g]]

    mine = slice(96, 96 + ROWS)

    def job_copy(i):
        to = lax.rem(me + i, NJ)
        return pltpu.make_async_remote_copy(
            src_ref=picked.at[to], dst_ref=txt.at[mine, my_columns],
            send_sem=route_send.at[1, i], recv_sem=route_recv.at[1],
            device_id={"job": to, "seq": z}, device_id_type=MESH,
        )

    @pl.loop(1, NJ)
    def _(i):
        job_copy(i).start()

    own_job = pltpu.make_async_copy(picked.at[me], txt.at[mine, my_columns], local_sem.at[0])
    own_job.start()

    flow_near(0)

    own_job.wait()
    arrive(picked.at[pl.ds(0, NJ - 1)], route_recv.at[1])
    halves = (slice(0, DT // 2), slice(DT // 2, DT))
    for p, cols in enumerate(halves):
        send(txt.at[96:160, cols], txt.at[32:96, cols], text_recv.at[p, 0], me, up)
        send(txt.at[96:160, cols], txt.at[160:224, cols], text_recv.at[p, 1], me, down)
    flow_far(0)
    flow_second(0, 0)
    for p, cols in enumerate(halves):
        arrive(txt.at[32:96, cols], text_recv.at[p, 0])
        send(txt.at[64:96, cols], txt.at[0:32, cols], text_recv.at[p, 2], me, up)
        arrive(txt.at[160:224, cols], text_recv.at[p, 1])
        send(txt.at[160:192, cols], txt.at[224:256, cols], text_recv.at[p, 3], me, down)
    flow_second(0, 1)
    flow_second(0, 2)
    flow_second(0, 3)
    flow_own(1)
    for index in range(4):
        flow_last(0, index)
    for p, cols in enumerate(halves):
        arrive(txt.at[0:32, cols], text_recv.at[p, 2])
        arrive(txt.at[224:256, cols], text_recv.at[p, 3])
    arrive(bias_far, bias_recv.at[0])
    flow_twin(0)

    def chunk(b, k):
        return hid.at[b, k * ROWS : (k + 1) * ROWS]

    def hid_send(b, k, way, hop, h):
        send(chunk(b, k), chunk(b, k - way), hid_recv.at[h, 0 if way == 1 else 1, hop, k], me, up if way == 1 else down)

    def hid_wait(b, k, way, hop, h):
        arrive(chunk(b, k - way), hid_recv.at[h, 0 if way == 1 else 1, hop, k])

    for h in range(2):
        acc[...] = jnp.zeros_like(acc)

        @pl.loop(0, 4)
        def _(i):
            at = pl.ds(pl.multiple_of(i * 1024, 1024), 1024)
            acc[...] += jnp.dot(txt[:, at], wt[h, at, :], preferred_element_type=jnp.float32)

        beside = (bias if h == 0 else bias_far)[0:1, 0:HB].astype(jnp.float32)
        for r in range(4):
            rows = slice(r * ROWS, (r + 1) * ROWS)
            hid[block(h), rows, :] = jax.nn.gelu(acc[rows, :] + beside, approximate=True).astype(jnp.bfloat16)
        for k in (3, 2, 1):
            hid_send(block(h), k, 1, 0, h)
            hid_send(block(h), 3 - k, -1, 0, h)

    def before(h, way, hop):
        return lax.rem(block(h) - way * hop + NZ, NZ)

    flow_near(1)
    for hop in (1, 2, 3):
        for h in range(2):
            for k in range(3, 0, -1):
                if k < hop:
                    continue
                for way in (1, -1):
                    src = (k - hop + 1) if way == 1 else 3 - (k - hop + 1)
                    b = before(h, way, hop)
                    hid_wait(b, src, way, hop - 1, h)
                    if k > hop:
                        hid_send(b, src - way, way, hop, h)
        if hop == 1:
            flow_far(1)
            flow_second(1, 0)
        if hop == 2:
            flow_second(1, 1)
            flow_second(1, 2)
            flow_second(1, 3)
            flow_own(2)
    for index in range(4):
        flow_last(1, index)
    flow_twin(1)
    flow_near(2)

    def project(whole, h, target, with_bias):
        acc[:, 0:KB] = jnp.zeros((WIN, KB), jnp.float32)

        @pl.loop(0, NZ)
        def _(b):
            at = pl.ds(pl.multiple_of(b * HB, 128), HB)
            acc[:, 0:KB] += jnp.dot(hid[b], whole[h, at, :], preferred_element_type=jnp.float32)

        total = acc[:, 0:KB]
        if with_bias:
            total = total + (bias if h == 0 else bias_far)[0:1, HB : HB + KB].astype(jnp.float32)
        target[z, h] = total.astype(jnp.bfloat16)

    def ring_send(target, sems, s, h):
        for way in (0, 1):
            if s < (4 if way == h else 3):
                origin = lax.rem(z + (NZ - s if way == 0 else s), NZ)
                ref = target.at[origin, h]
                send(ref, ref, sems.at[way, s, h], me, up if way == 0 else down)

    def ring_wait(target, sems, s, h):
        for way in (0, 1):
            if s <= (4 if way == h else 3):
                origin = lax.rem(z + (NZ - s if way == 0 else s), NZ)
                arrive(target.at[origin, h], sems.at[way, s - 1, h])

    def ring_step(target, sems, s):
        for h in range(2):
            ring_wait(target, sems, s, h)
            if s < 4:
                ring_send(target, sems, s, h)

    for h in range(2):
        project(wk, h, kall, False)
        ring_send(kall, key_recv, 0, h)
    flow_far(2)
    flow_second(2, 0)
    ring_step(kall, key_recv, 1)
    flow_second(2, 1)
    flow_second(2, 2)
    flow_second(2, 3)
    ring_step(kall, key_recv, 2)
    for index in range(4):
        flow_last(2, index)
    ring_step(kall, key_recv, 3)
    flow_twin(2)
    for h in range(2):
        project(wv, h, vall, True)
        ring_send(vall, value_recv, 0, h)
    ring_step(kall, key_recv, 4)
    for copy in fetch:
        copy.wait()

    live = text_len[me]
    scale = HD ** (-0.5)

    def dead(origin):
        at = lax.broadcasted_iota(jnp.int32, (1, WIN), 1) + (ROWS * origin - 96)
        at = jnp.where(at < 0, at + TXT, jnp.where(at >= TXT, at - TXT, at))
        return jnp.where(at < live, jnp.float32(0), jnp.float32(-1e30))

    NT = (((1,), (1,)), ((), ()))

    def weigh(q):
        @pl.loop(0, 2)
        def _(n):
            b = lax.rem(q + 4 * n, NZ)
            other = lax.rem(b + 4, NZ)
            off_a, off_b = dead(b), dead(other)
            for i in range(KB // HD):
                cols = slice(i * HD, (i + 1) * HD)
                ahead = qv[b, :, cols]
                sa = lax.dot_general(ahead, kall[b, 0, :, cols], NT, preferred_element_type=jnp.float32) * scale + off_a
                sb = lax.dot_general(ahead, kall[other, 1, :, cols], NT, preferred_element_type=jnp.float32) * scale + off_b
                peak = jnp.maximum(jnp.max(sa, axis=1, keepdims=True), jnp.max(sb, axis=1, keepdims=True))
                ea, eb = jnp.exp(sa - peak), jnp.exp(sb - peak)
                share_of = 1.0 / (jnp.sum(ea, axis=1, keepdims=True) + jnp.sum(eb, axis=1, keepdims=True))
                prob[b, i, :, 0:WIN] = (ea * share_of).astype(jnp.bfloat16)
                prob[b, i, :, WIN:TXT] = (eb * share_of).astype(jnp.bfloat16)

    def mix(q):
        @pl.loop(0, 2)
        def _(n):
            b = lax.rem(q + 4 * n, NZ)
            other = lax.rem(b + 4, NZ)
            for i in range(KB // HD):
                cols = slice(i * HD, (i + 1) * HD)
                total = jnp.dot(prob[b, i, :, 0:WIN], vall[b, 0, :, cols], preferred_element_type=jnp.float32)
                total += jnp.dot(prob[b, i, :, WIN:TXT], vall[other, 1, :, cols], preferred_element_type=jnp.float32)
                ov[b, :, cols] = total.astype(jnp.bfloat16)

    def quarter(d):
        return lax.rem(z + d, 4)

    weigh(quarter(2))
    ring_step(vall, value_recv, 1)
    weigh(quarter(1))
    ring_step(vall, value_recv, 2)
    weigh(quarter(3))
    weigh(quarter(0))
    ring_step(vall, value_recv, 3)
    mix(quarter(2))
    mix(quarter(1))
    mix(quarter(3))
    ring_step(vall, value_recv, 4)
    mix(quarter(0))
    store = [
        pltpu.make_async_copy(ov.at[b], out_hbm.at[0, :, pl.ds(b * KB, KB)], query_sem.at[b])
        for b in range(NZ)
    ]
    for copy in store:
        copy.start()
    for copy in store:
        copy.wait()

    for copy in pending:
        copy.wait_send()
    for copy in first:
        pl.when(core == 1)(copy.wait_send)

    @pl.loop(1, NJ)
    def _(i):
        slab_copy(i).wait_send()
        job_copy(i).wait_send()


def body(text_cache, source, text_len, query, w_text, b_text, w_key, w_value, b_value):
    bf16, dma = jnp.bfloat16, pltpu.SemaphoreType.DMA
    bias = jnp.broadcast_to(jnp.concatenate([b_text, b_value])[None], (16, HB + KB))
    whole, smem, vmem = (pl.BlockSpec(memory_space=s) for s in (pl.ANY, pltpu.SMEM, pltpu.VMEM))
    return pl.pallas_call(
        kernel,
        out_shape=jax.ShapeDtypeStruct((1, VR, HQ), bf16),
        in_specs=[whole, smem, smem, whole, whole, whole, whole, vmem],
        out_specs=whole,
        scratch_shapes=[
            pltpu.VMEM((2 * NJ, ROWS, 128), bf16),
            pltpu.VMEM((NJ, ROWS, 128), bf16),
            pltpu.VMEM((WIN, DT), bf16),
            pltpu.VMEM((2, DT, HB), bf16),
            pltpu.VMEM((2, DM, KB), bf16),
            pltpu.VMEM((2, DM, KB), bf16),
            pltpu.VMEM((NZ, WIN, HB), bf16),
            pltpu.VMEM((NZ, 2, WIN, KB), bf16),
            pltpu.VMEM((NZ, 2, WIN, KB), bf16),
            pltpu.VMEM((NZ, KB // HD, VR, TXT), bf16),
            pltpu.VMEM((NZ, VR, KB), bf16),
            pltpu.VMEM((NZ, VR, KB), bf16),
            pltpu.VMEM((16, HB + KB), bf16),
            pltpu.VMEM((WIN, HB), jnp.float32),
            dma((N_SEND,)),
            dma((2, NJ)),
            dma((2,)),
            dma((4,)),
            dma((3, 2)),
            dma((3, 20)),
            dma((3,)),
            dma((2, 4)),
            dma((2, 2, 3, 4)),
            dma((2, 4, 2)),
            dma((2, 4, 2)),
            dma((1,)),
            dma((NZ,)),
        ],
        compiler_params=pltpu.CompilerParams(
            collective_id=0, has_side_effects=True, vmem_limit_bytes=60 * 2**20
        ),
    )(text_cache, source, text_len, query, w_text, w_key, w_value, bias)


def solution(mesh):
    in_specs = (
        P("job", None, "seq", None),
        P(),
        P(),
        P("job", "seq", None),
        P("job", "seq"),
        P("seq"),
        P("job", "seq"),
        P("job", "seq"),
        P("seq"),
    )
    out_specs = P("job", "seq", None)
    return jax.shard_map(body, mesh=mesh, in_specs=in_specs, out_specs=out_specs, check_vma=False)
```

time: 444 us -> 177 us (0.40)
  waiting for transfers between devices: 348 us -> 0 us
  Pallas kernels: 0 us -> 173 us
  matrix products: 33.4 us -> 0 us
  blocking collectives: 15.4 us -> 0 us
  between operations: 13.6 us -> 0.01 us
  local copies, waits for them, and re-layouts: 13.7 us -> 3.27 us
  starting transfers between devices: 9.05 us -> 0 us
  other arithmetic: 9.71 us -> 0.71 us
    all_gather x7 -> x0, waiting for transfers between devices: 329 us -> none  [the longest x1 65.4 us: body(): hidden = lax.all_gather(hidden_part, 'seq', axis=1, tiled=True)]
    pallas_call x0 -> x1, Pallas kernels: none -> 173 us  [body(): pl.pallas_call(kernel, out_shape=jax.ShapeDtypeStruct((1, VR, HQ), bf16),...]
    dot_general x5 -> x0, matrix products: 33.4 us -> none  [the longest x3 22.9 us: add_product(): return jnp.dot(left, portion, preferred_element_type=jnp.float32)]
    all_to_all x1 -> x0, waiting for transfers between devices: 16.8 us -> none  [body(): lax.all_to_all(cached.reshape(slot_count, groups, portion_rows, text_widt...]
    all_to_all x1 -> x0, blocking collectives: 15.4 us -> none  [body(): lax.all_to_all(picked, 'job', split_axis=0, concat_axis=0, tiled=True)]
    sub x1 -> x0, other arithmetic: 9.05 us -> none  [attend(): exponent = jnp.exp(scores - row_peak)]
    all_to_all x1 -> x0, starting transfers between devices: 8.59 us -> none  [body(): lax.all_to_all(cached.reshape(slot_count, groups, portion_rows, text_widt...]
    another operation x2 -> x0, local copies, waits for them, and re-layouts: 4.65 us -> none  [the longest x1 2.58 us: body(): return result[None]]
  transfers between devices with their start and end apart: 8 -> 0, of which waited for: 8 -> 0; matrix products, arithmetic and copies ran while one was open for 8% -> 0% of each run, Pallas kernels for 0% -> 0%
where the time goes in v1:
time: 177 us
  Pallas kernels  173 us (98%)
  local copies, waits for them, and re-layouts  3.27 us (2%)
    pallas_call x1, Pallas kernels, body(): pl.pallas_call(kernel, out_shape=jax.ShapeDtypeStruct((1, VR, HQ), bf16),...  173 us

profile of v1, /device:TPU:1, one launch (start us, length us, event | category | flops | bytes accessed | tf_op | source)
XLA Modules:
  0.0 177.3 jit_solution(16926246358627617069)
XLA Ops:
  0.0 0.7 pad_maximum_fusion
  0.7 0.6 broadcast_in_dim.2.bias
  1.3 173.3 %shard_map.91 = bf16[1,256,3072]{2,1,0:T(8,128)(2,1)} custom-call(bf16[1,2,64,4096]{3,2,1,0:T(8,128)(2,1)} %cache.1, s32[32]{0:T(128)} %source.1, s32[32]{0:T(128)} %text_len.1, bf16[1,256,3072]{2,1,0:T(8,128)(2,1)} %query.1, bf16[128,640]{1,0:T(8,128)(2,1)} %w_text.1, bf16[160,384]{1,0:T(8,128)(2,1)} %w_key.1, bf16[160,384]{1,0:T(8,128)(2,1)} %w_value.1, ...), custom_call_target="tpu_custom_call" | custom-call | tf_op jit(solution)/shard_map/pallas_call | solution.py:408
  174.6 2.7 %copy.11 = bf16[1,256,3072]{2,1,0:T(8,128)(2,1)} copy(bf16[1,256,3072]{2,1,0:T(8,128)(2,1)} %shard_map.91) | data formatting | bytes 3145728

commit v2 on v1

v2 whole, which is shorter than its diff:
```python
import functools

import jax
import jax.numpy as jnp
from jax import lax
from jax.experimental import pallas as pl
from jax.experimental.pallas import tpu as pltpu
from jax.sharding import PartitionSpec as P

MESH = pl.DeviceIdType.MESH
HD = 128
NJ, NZ, NX = 32, 8, 4
TXT, DT, DM, HQ, VR = 512, 4096, 5120, 3072, 256
ROWS = TXT // NZ
HB, KB = DM // NZ, HQ // NZ
WIN = 256
DEPTHS = (DT // NJ, DM // NJ, DM // NJ)
HALF = ROWS // 2
N_SEND = 320


def kernel(
    cache, source, text_len, query, w_text, w_key, w_value, b_text, b_value, out,
    slabs_a, slabs_b, picked, txt, wt, wk, wv, hid, kall, vall, prob, qv, bias, bias_far, acc,
    send_sem, route_send, route_recv, local_sem, start_recv, flow_recv, twin_recv,
    text_recv, hid_recv, key_recv, value_recv, bias_recv, query_sem,
):
    me, z = lax.axis_index("job"), lax.axis_index("seq")
    core, chip = lax.rem(me, 2), me // 2
    x, y = chip // NX, lax.rem(chip, NX)
    u, v = jnp.where(core == 0, x, y), jnp.where(core == 0, y, x)
    step_u, step_v = 8 - 6 * core, 2 + 6 * core
    up, down, far = lax.rem(z + 1, NZ), lax.rem(z + NZ - 1, NZ), lax.rem(z + 4, NZ)
    twin = me + 1 - 2 * core

    def block(h):
        return z if h == 0 else far

    def at_uv(a, b):
        return lax.rem(u + a + NX, NX) * step_u + lax.rem(v + b + NX, NX) * step_v

    pending = []

    def send(src, dst, recv, job, seq):
        n = len(pending)
        copy = pltpu.make_async_remote_copy(
            src_ref=src, dst_ref=dst, send_sem=send_sem.at[n], recv_sem=recv,
            device_id={"job": job, "seq": seq}, device_id_type=MESH,
        )
        copy.start()
        pending.append(copy)

    def arrive(ref, sem):
        pltpu.make_async_copy(ref, ref, sem).wait()

    barrier = pltpu.get_barrier_semaphore()

    def greet(job, seq):
        pl.semaphore_signal(barrier, inc=1, device_id={"job": job, "seq": seq}, device_id_type=MESH)

    @pl.loop(1, NJ)
    def _(i):
        greet(lax.rem(me + i, NJ), z)

    greet(me, up)
    greet(me, down)
    greet(me, far)
    greet(twin, far)
    pl.semaphore_wait(barrier, NJ - 1 + 4)

    slabs = (slabs_a, slabs_b)

    def slab_copy(p, i):
        to = lax.rem(me + i, NJ)
        return pltpu.make_async_remote_copy(
            src_ref=cache.at[0, :, p * HALF : (p + 1) * HALF, pl.ds(pl.multiple_of(to * 128, 128), 128)],
            dst_ref=slabs[p].at[pl.ds(2 * me, 2)],
            send_sem=route_send.at[0, p, i], recv_sem=route_recv.at[0, p],
            device_id={"job": to, "seq": z}, device_id_type=MESH,
        )

    my_columns = pl.ds(pl.multiple_of(me * 128, 128), 128)
    own_slab = [
        pltpu.make_async_copy(
            cache.at[0, :, p * HALF : (p + 1) * HALF, my_columns],
            slabs[p].at[pl.ds(2 * me, 2)],
            local_sem.at[p],
        )
        for p in range(2)
    ]
    for p in range(2):

        @pl.loop(1, NJ)
        def _(i):
            slab_copy(p, i).start()

        own_slab[p].start()

    weights = ((w_text, wt), (w_key, wk), (w_value, wv))
    keeps = [
        pltpu.make_async_copy(shard, whole.at[0, me], start_recv.at[t, 0])
        for t, (shard, whole) in enumerate(weights)
    ]
    for t, (shard, whole) in enumerate(weights):
        keeps[t].start()
        send(shard, whole.at[1, me], start_recv.at[t, 1], me, far)
    bias[:, 0:HB] = jnp.broadcast_to(b_text[...].astype(jnp.float32), (16, HB)).astype(jnp.bfloat16)
    bias[:, HB : HB + KB] = jnp.broadcast_to(b_value[...].astype(jnp.float32), (16, KB)).astype(jnp.bfloat16)
    send(bias, bias_far, bias_recv.at[0], me, far)
    fetch = [
        pltpu.make_async_copy(query.at[0, :, pl.ds(b * KB, KB)], qv.at[b], query_sem.at[b])
        for b in range(NZ)
    ]
    for copy in fetch:
        copy.start()

    def piece(t, h, a, b, part=None):
        ref = weights[t][1].at[h, at_uv(a, b) + core]
        if part is None:
            return ref
        n = DEPTHS[t] // 2
        return ref.at[pl.ds(part * n, n)]

    def give(t, h, a, b, da, db, slot, part=None):
        ref = piece(t, h, a, b, part)
        send(ref, ref, flow_recv.at[t, h, slot], at_uv(da, db) + core, z)

    def share(t, h, a, b):
        ref = piece(t, h, a, b)
        send(ref, ref, twin_recv.at[t, h], twin, z)

    def across(t, h, a, index):
        give(t, h, a, 0, 0, 1, 4 + 4 * index)
        give(t, h, a, 0, 0, -1, 5 + 4 * index)
        share(t, h, a, 0)

    def flow_own(t, h):
        arrive(weights[t][1].at[h, me], start_recv.at[t, h])
        give(t, h, 0, 0, 1, 0, 0)
        give(t, h, 0, 0, -1, 0, 1)
        across(t, h, 0, 0)

    def flow_near(t, h):
        arrive(piece(t, h, -1, 0), flow_recv.at[t, h, 0])
        give(t, h, -1, 0, 1, 0, 2, 0)
        across(t, h, -1, 1)
        arrive(piece(t, h, 1, 0), flow_recv.at[t, h, 1])
        give(t, h, 1, 0, -1, 0, 3, 1)
        across(t, h, 1, 2)

    def flow_far(t, h):
        arrive(piece(t, h, 2, 0, 0), flow_recv.at[t, h, 2])
        arrive(piece(t, h, 2, 0, 1), flow_recv.at[t, h, 3])
        across(t, h, 2, 3)

    PLACES = (0, -1, 1, 2)

    def flow_second(t, h, *indices):
        for index in indices:
            a = PLACES[index]
            arrive(piece(t, h, a, -1), flow_recv.at[t, h, 4 + 4 * index])
            give(t, h, a, -1, 0, 1, 6 + 4 * index, 0)
            share(t, h, a, -1)
            arrive(piece(t, h, a, 1), flow_recv.at[t, h, 5 + 4 * index])
            give(t, h, a, 1, 0, -1, 7 + 4 * index, 1)
            share(t, h, a, 1)

    def flow_last(t, h):
        for index, a in enumerate(PLACES):
            arrive(piece(t, h, a, 2, 0), flow_recv.at[t, h, 6 + 4 * index])
            arrive(piece(t, h, a, 2, 1), flow_recv.at[t, h, 7 + 4 * index])
            share(t, h, a, 2)

    def flow_twin(t, h):
        arrive(weights[t][1].at[h, 0 : NJ // 2], twin_recv.at[t, h])

    def first_row(p):
        return 96 + p * HALF

    def job_copy(p, i):
        to = lax.rem(me + i, NJ)
        return pltpu.make_async_remote_copy(
            src_ref=picked.at[p, to], dst_ref=txt.at[first_row(p) : first_row(p) + HALF, my_columns],
            send_sem=route_send.at[1, p, i], recv_sem=route_recv.at[1, p],
            device_id={"job": to, "seq": z}, device_id_type=MESH,
        )

    own_job = [
        pltpu.make_async_copy(
            picked.at[p, me], txt.at[first_row(p) : first_row(p) + HALF, my_columns], local_sem.at[p]
        )
        for p in range(2)
    ]

    def route_on(p):
        own_slab[p].wait()
        arrive(slabs[p].at[pl.ds(0, 2 * (NJ - 1))], route_recv.at[0, p])

        @pl.loop(0, NJ)
        def _(g):
            picked[p, g] = slabs[p][source[g]]

        @pl.loop(1, NJ)
        def _(i):
            job_copy(p, i).start()

        own_job[p].start()

    def lines(p, way, hops):
        at = first_row(p) - way * hops * ROWS
        return txt.at[at : at + HALF]

    def text_on(p):
        own_job[p].wait()
        arrive(picked.at[p, pl.ds(0, NJ - 1)], route_recv.at[1, p])
        for way in (2 * p - 1, 1 - 2 * p):
            send(lines(p, way, 0), lines(p, way, 1), text_recv.at[p, (1 + way) // 2], me, up if way == 1 else down)

    def text_pass(p):
        way = 2 * p - 1
        arrive(lines(p, way, 1), text_recv.at[p, (1 + way) // 2])
        send(lines(p, way, 1), lines(p, way, 2), text_recv.at[p, 2], me, up if way == 1 else down)

    def text_last(p):
        way = 2 * p - 1
        arrive(lines(p, -way, 1), text_recv.at[p, (1 - way) // 2])
        arrive(lines(p, way, 2), text_recv.at[p, 2])

    flow_own(0, 0)
    route_on(0)
    flow_near(0, 0)
    route_on(1)
    flow_own(0, 1)
    flow_far(0, 0)
    flow_second(0, 0, 0)
    text_on(0)
    flow_second(0, 0, 1, 2)
    flow_near(0, 1)
    text_on(1)
    text_pass(0)
    flow_second(0, 0, 3)
    flow_far(0, 1)
    flow_second(0, 1, 0)
    text_pass(1)
    flow_last(0, 0)
    flow_second(0, 1, 1, 2, 3)
    flow_own(1, 0)
    text_last(0)
    text_last(1)
    flow_twin(0, 0)

    def chunk(b, k):
        return hid.at[b, k * ROWS : (k + 1) * ROWS]

    def hid_send(b, k, way, hop, h):
        send(chunk(b, k), chunk(b, k - way), hid_recv.at[h, 0 if way == 1 else 1, hop, k], me, up if way == 1 else down)

    def hid_wait(b, k, way, hop, h):
        arrive(chunk(b, k - way), hid_recv.at[h, 0 if way == 1 else 1, hop, k])

    def embed(h):
        acc[...] = jnp.zeros_like(acc)

        @pl.loop(0, 4)
        def _(i):
            at = pl.ds(pl.multiple_of(i * 1024, 1024), 1024)
            part = wt[h, pl.ds(i * 8, 8)].reshape(1024, HB)
            acc[...] += jnp.dot(txt[:, at], part, preferred_element_type=jnp.float32)

        beside = (bias if h == 0 else bias_far)[0:1, 0:HB].astype(jnp.float32)
        for r in range(4):
            rows = slice(r * ROWS, (r + 1) * ROWS)
            hid[block(h), rows, :] = jax.nn.gelu(acc[rows, :] + beside, approximate=True).astype(jnp.bfloat16)
        for k in (3, 2, 1):
            hid_send(block(h), k, 1, 0, h)
            hid_send(block(h), 3 - k, -1, 0, h)

    def hid_pass(h, hop):
        for k in range(3, hop - 1, -1):
            for way in (1, -1):
                src = (k - hop + 1) if way == 1 else 3 - (k - hop + 1)
                b = lax.rem(block(h) - way * hop + NZ, NZ)
                hid_wait(b, src, way, hop - 1, h)
                if k > hop:
                    hid_send(b, src - way, way, hop, h)

    def project(whole, h, target, with_bias):
        acc[:, 0:KB] = jnp.zeros((WIN, KB), jnp.float32)

        @pl.loop(0, NZ)
        def _(b):
            part = whole[h, pl.ds(b * 4, 4)].reshape(HB, KB)
            acc[:, 0:KB] += jnp.dot(hid[b], part, preferred_element_type=jnp.float32)

        total = acc[:, 0:KB]
        if with_bias:
            total = total + (bias if h == 0 else bias_far)[0:1, HB : HB + KB].astype(jnp.float32)
        target[z, h] = total.astype(jnp.bfloat16)

    def ring_send(target, sems, s, h):
        for way in (0, 1):
            if s < (4 if way == h else 3):
                origin = lax.rem(z + (NZ - s if way == 0 else s), NZ)
                ref = target.at[origin, h]
                send(ref, ref, sems.at[way, s, h], me, up if way == 0 else down)

    def ring_wait(target, sems, s, h):
        for way in (0, 1):
            if s <= (4 if way == h else 3):
                origin = lax.rem(z + (NZ - s if way == 0 else s), NZ)
                arrive(target.at[origin, h], sems.at[way, s - 1, h])

    def ring_step(target, sems, s):
        for h in range(2):
            ring_wait(target, sems, s, h)
            if s < 4:
                ring_send(target, sems, s, h)

    embed(0)
    flow_last(0, 1)
    flow_near(1, 0)
    hid_pass(0, 1)
    flow_own(1, 1)
    flow_far(1, 0)
    flow_second(1, 0, 0)
    arrive(bias_far, bias_recv.at[0])
    flow_twin(0, 1)
    embed(1)
    hid_pass(0, 2)
    flow_second(1, 0, 1, 2)
    hid_pass(1, 1)
    flow_near(1, 1)
    hid_pass(0, 3)
    flow_second(1, 0, 3)
    hid_pass(1, 2)
    flow_far(1, 1)
    flow_second(1, 1, 0)
    hid_pass(1, 3)
    flow_last(1, 0)
    flow_second(1, 1, 1, 2, 3)
    flow_own(2, 0)
    flow_twin(1, 0)
    project(wk, 0, kall, False)
    ring_send(kall, key_recv, 0, 0)
    flow_last(1, 1)
    flow_near(2, 0)
    flow_own(2, 1)
    flow_twin(1, 1)
    project(wk, 1, kall, False)
    ring_send(kall, key_recv, 0, 1)
    flow_far(2, 0)
    flow_second(2, 0, 0)
    ring_step(kall, key_recv, 1)
    flow_second(2, 0, 1, 2)
    flow_near(2, 1)
    ring_step(kall, key_recv, 2)
    flow_second(2, 0, 3)
    flow_far(2, 1)
    flow_second(2, 1, 0)
    ring_step(kall, key_recv, 3)
    flow_last(2, 0)
    flow_second(2, 1, 1, 2, 3)
    flow_twin(2, 0)
    project(wv, 0, vall, True)
    ring_send(vall, value_recv, 0, 0)
    flow_last(2, 1)
    ring_step(kall, key_recv, 4)
    flow_twin(2, 1)
    project(wv, 1, vall, True)
    ring_send(vall, value_recv, 0, 1)
    for copy in fetch:
        copy.wait()

    live = text_len[me]
    scale = HD ** (-0.5)

    def dead(origin):
        at = lax.broadcasted_iota(jnp.int32, (1, WIN), 1) + (ROWS * origin - 96)
        at = jnp.where(at < 0, at + TXT, jnp.where(at >= TXT, at - TXT, at))
        return jnp.where(at < live, jnp.float32(0), jnp.float32(-1e30))

    NT = (((1,), (1,)), ((), ()))

    def weigh(q):
        @pl.loop(0, 2)
        def _(n):
            b = lax.rem(q + 4 * n, NZ)
            other = lax.rem(b + 4, NZ)
            off_a, off_b = dead(b), dead(other)
            for i in range(KB // HD):
                cols = slice(i * HD, (i + 1) * HD)
                ahead = qv[b, :, cols]
                sa = lax.dot_general(ahead, kall[b, 0, :, cols], NT, preferred_element_type=jnp.float32) * scale + off_a
                sb = lax.dot_general(ahead, kall[other, 1, :, cols], NT, preferred_element_type=jnp.float32) * scale + off_b
                peak = jnp.maximum(jnp.max(sa, axis=1, keepdims=True), jnp.max(sb, axis=1, keepdims=True))
                ea, eb = jnp.exp(sa - peak), jnp.exp(sb - peak)
                share_of = 1.0 / (jnp.sum(ea, axis=1, keepdims=True) + jnp.sum(eb, axis=1, keepdims=True))
                prob[b, i, :, 0:WIN] = (ea * share_of).astype(jnp.bfloat16)
                prob[b, i, :, WIN:TXT] = (eb * share_of).astype(jnp.bfloat16)

    def mix(q):
        @pl.loop(0, 2)
        def _(n):
            b = lax.rem(q + 4 * n, NZ)
            other = lax.rem(b + 4, NZ)
            for i in range(KB // HD):
                cols = slice(i * HD, (i + 1) * HD)
                total = jnp.dot(prob[b, i, :, 0:WIN], vall[b, 0, :, cols], preferred_element_type=jnp.float32)
                total += jnp.dot(prob[b, i, :, WIN:TXT], vall[other, 1, :, cols], preferred_element_type=jnp.float32)
                out[0, :, pl.ds(pl.multiple_of(b * KB + i * HD, HD), HD)] = total.astype(jnp.bfloat16)

    def quarter(d):
        return lax.rem(z + d, 4)

    weigh(quarter(2))
    ring_step(vall, value_recv, 1)
    weigh(quarter(1))
    ring_step(vall, value_recv, 2)
    weigh(quarter(3))
    weigh(quarter(0))
    ring_step(vall, value_recv, 3)
    mix(quarter(2))
    mix(quarter(1))
    mix(quarter(3))
    ring_step(vall, value_recv, 4)
    mix(quarter(0))

    for copy in pending:
        copy.wait_send()
    for p in range(2):

        @pl.loop(1, NJ)
        def _(i):
            slab_copy(p, i).wait_send()
            job_copy(p, i).wait_send()


def body(text_cache, source, text_len, query, w_text, b_text, w_key, w_value, b_value):
    bf16, dma = jnp.bfloat16, pltpu.SemaphoreType.DMA
    whole, smem, vmem = (pl.BlockSpec(memory_space=s) for s in (pl.ANY, pltpu.SMEM, pltpu.VMEM))
    return pl.pallas_call(
        kernel,
        out_shape=pltpu.VMEM((1, VR, HQ), bf16),
        in_specs=[whole, smem, smem, whole, whole, whole, whole, vmem, vmem],
        out_specs=vmem,
        scratch_shapes=[
            pltpu.VMEM((2 * NJ, HALF, 128), bf16),
            pltpu.VMEM((2 * NJ, HALF, 128), bf16),
            pltpu.VMEM((2, NJ, HALF, 128), bf16),
            pltpu.VMEM((WIN, DT), bf16),
            pltpu.VMEM((2, NJ, DT // NJ, HB), bf16),
            pltpu.VMEM((2, NJ, DM // NJ, KB), bf16),
            pltpu.VMEM((2, NJ, DM // NJ, KB), bf16),
            pltpu.VMEM((NZ, WIN, HB), bf16),
            pltpu.VMEM((NZ, 2, WIN, KB), bf16),
            pltpu.VMEM((NZ, 2, WIN, KB), bf16),
            pltpu.VMEM((NZ, KB // HD, VR, TXT), bf16),
            pltpu.VMEM((NZ, VR, KB), bf16),
            pltpu.VMEM((16, HB + KB), bf16),
            pltpu.VMEM((16, HB + KB), bf16),
            pltpu.VMEM((WIN, HB), jnp.float32),
            dma((N_SEND,)),
            dma((2, 2, NJ)),
            dma((2, 2)),
            dma((2,)),
            dma((3, 2)),
            dma((3, 2, 20)),
            dma((3, 2)),
            dma((2, 3)),
            dma((2, 2, 3, 4)),
            dma((2, 4, 2)),
            dma((2, 4, 2)),
            dma((1,)),
            dma((NZ,)),
        ],
        compiler_params=pltpu.CompilerParams(
            collective_id=0, has_side_effects=True, vmem_limit_bytes=56 * 2**20
        ),
    )(text_cache, source, text_len, query, w_text, w_key, w_value, b_text[None], b_value[None])


def solution(mesh):
    in_specs = (
        P("job", None, "seq", None),
        P(),
        P(),
        P("job", "seq", None),
        P("job", "seq"),
        P("seq"),
        P("job", "seq"),
        P("job", "seq"),
        P("seq"),
    )
    out_specs = P("job", "seq", None)
    return jax.shard_map(body, mesh=mesh, in_specs=in_specs, out_specs=out_specs, check_vma=False)
```

time: 177 us -> 169 us (0.955)
  Pallas kernels: 173 us -> 165 us
    pallas_call x1, Pallas kernels: 173 us -> 165 us  [body(): pl.pallas_call(kernel, out_shape=pltpu.VMEM((1, VR, HQ), bf16), in_specs=...]
    broadcast_in_dim x1 -> x2, local copies, waits for them, and re-layouts: 0.62 us -> 2.53 us  [the longest x1 1.27 us: body(): b_value[None]]
where the time goes in v2:
time: 169 us
  Pallas kernels  165 us (98%)
  local copies, waits for them, and re-layouts  3.68 us (2%)
    pallas_call x1, Pallas kernels, body(): pl.pallas_call(kernel, out_shape=pltpu.VMEM((1, VR, HQ), bf16), in_specs=...  165 us

profile of v2, /device:TPU:1, one launch (start us, length us, event | category | flops | bytes accessed | tf_op | source)
XLA Modules:
  0.0 169.0 jit_solution(3002072069801765834)
XLA Ops:
  0.0 1.3 broadcast_in_dim.7.b_value
  1.3 1.3 broadcast_in_dim.6.b_text
  2.5 165.3 %shard_map.91 = bf16[1,256,3072]{2,1,0:T(8,128)(2,1)S(1)} custom-call(bf16[1,2,64,4096]{3,2,1,0:T(8,128)(2,1)} %cache.1, s32[32]{0:T(128)} %source.1, s32[32]{0:T(128)} %text_len.1, bf16[1,256,3072]{2,1,0:T(8,128)(2,1)} %query.1, bf16[128,640]{1,0:T(8,128)(2,1)} %w_text.1, bf16[160,384]{1,0:T(8,128)(2,1)} %w_key.1, bf16[160,384]{1,0:T(8,128)(2,1)} %w_value.1, ...), custom_call_target="tpu_custom_call" | custom-call | tf_op jit(solution)/shard_map/pallas_call | solution.py:441
  167.8 1.1 copy.11

commit v3 on v2

--- a/solution.py
+++ b/solution.py
@@ -17,6 +17,44 @@
 DEPTHS = (DT // NJ, DM // NJ, DM // NJ)
 HALF = ROWS // 2
 N_SEND = 320
+STEPS = (
+    ("route_on", 0), ("own", 0, 0), ("route_on", 1), ("near", 0, 0, -1), ("near", 0, 0, 1), ("text_on", 0),
+    ("second", 0, 0, 0, -1), ("second", 0, 0, 0, 1), ("own", 0, 1), ("second", 0, 0, 1, 1), ("text_on", 1),
+    ("far", 0, 0), ("second", 0, 0, 1, -1), ("text_pass", 0), ("second", 0, 0, 2, 1), ("second", 0, 0, 2, -1),
+    ("last", 0, 0, 0), ("near", 0, 1, 1), ("near", 0, 1, -1), ("second", 0, 1, 0, 1), ("second", 0, 1, 0, -1),
+    ("text_pass", 1), ("second", 0, 0, 3, -1), ("second", 0, 0, 3, 1), ("last", 0, 0, 1), ("last", 0, 0, 2),
+    ("second", 0, 1, 2, -1), ("second", 0, 1, 2, 1), ("far", 0, 1), ("second", 0, 1, 1, 1),
+    ("second", 0, 1, 1, -1), ("last", 0, 1, 0), ("own", 1, 0), ("last", 0, 0, 3), ("last", 0, 1, 2),
+    ("own", 1, 1), ("embed", 0), ("second", 0, 1, 3, -1), ("second", 0, 1, 3, 1), ("last", 0, 1, 1),
+    ("near", 1, 0, -1), ("near", 1, 0, 1), ("second", 1, 0, 0, 1), ("second", 1, 0, 0, -1), ("near", 1, 1, 1),
+    ("near", 1, 1, -1), ("second", 1, 1, 0, 1), ("second", 1, 1, 0, -1), ("hid", 0, 1, 3, 1),
+    ("hid", 0, 1, 3, -1), ("last", 0, 1, 3), ("hid", 0, 1, 2, 1), ("hid", 0, 1, 2, -1),
+    ("second", 1, 0, 1, 1), ("far", 1, 0), ("second", 1, 0, 1, -1), ("embed", 1), ("hid", 0, 2, 3, 1),
+    ("hid", 0, 2, 3, -1), ("hid", 0, 1, 1, 1), ("hid", 0, 1, 1, -1), ("second", 1, 0, 2, -1),
+    ("second", 1, 0, 2, 1), ("last", 1, 0, 0), ("second", 1, 1, 2, -1), ("second", 1, 1, 2, 1), ("far", 1, 1),
+    ("hid", 0, 2, 2, 1), ("hid", 0, 2, 2, -1), ("second", 1, 1, 1, 1), ("second", 1, 1, 1, -1),
+    ("last", 1, 1, 0), ("hid", 1, 1, 3, 1), ("hid", 1, 1, 3, -1), ("own", 2, 0), ("second", 1, 0, 3, -1),
+    ("second", 1, 0, 3, 1), ("last", 1, 0, 1), ("last", 1, 0, 2), ("hid", 1, 1, 2, 1), ("hid", 1, 1, 2, -1),
+    ("last", 1, 1, 2), ("own", 2, 1), ("hid", 1, 1, 1, 1), ("hid", 1, 1, 1, -1), ("second", 1, 1, 3, -1),
+    ("second", 1, 1, 3, 1), ("last", 1, 1, 1), ("hid", 0, 3, 3, 1), ("hid", 0, 3, 3, -1), ("near", 2, 0, 1),
+    ("near", 2, 0, -1), ("second", 2, 0, 0, 1), ("second", 2, 0, 0, -1), ("hid", 1, 2, 3, 1),
+    ("hid", 1, 2, 3, -1), ("last", 1, 0, 3), ("hid", 1, 2, 2, 1), ("near", 2, 1, 1), ("hid", 1, 2, 2, -1),
+    ("near", 2, 1, -1), ("second", 2, 1, 0, 1), ("second", 2, 1, 0, -1), ("last", 1, 1, 3),
+    ("hid", 1, 3, 3, 1), ("hid", 1, 3, 3, -1), ("project", 1, 0), ("project", 1, 1), ("far", 2, 0),
+    ("second", 2, 0, 1, -1), ("second", 2, 0, 1, 1), ("second", 2, 0, 2, -1), ("second", 2, 0, 2, 1),
+    ("last", 2, 0, 0), ("second", 2, 1, 2, -1), ("second", 2, 1, 2, 1), ("far", 2, 1), ("second", 2, 1, 1, 1),
+    ("second", 2, 1, 1, -1), ("last", 2, 1, 0), ("ring", 1, 1, 0, 0), ("ring", 1, 1, 0, 1),
+    ("second", 2, 0, 3, 1), ("second", 2, 0, 3, -1), ("last", 2, 0, 1), ("last", 2, 0, 2), ("last", 2, 1, 2),
+    ("second", 2, 1, 3, 1), ("second", 2, 1, 3, -1), ("ring", 1, 1, 1, 0), ("ring", 1, 1, 1, 1),
+    ("last", 2, 1, 1), ("last", 2, 0, 3), ("last", 2, 1, 3), ("project", 2, 0), ("ring", 1, 2, 0, 0),
+    ("ring", 1, 2, 0, 1), ("project", 2, 1), ("ring", 1, 2, 1, 0), ("ring", 1, 2, 1, 1), ("weigh", 2),
+    ("ring", 2, 1, 0, 0), ("ring", 2, 1, 0, 1), ("ring", 1, 3, 0, 0), ("ring", 1, 3, 0, 1),
+    ("ring", 2, 1, 1, 0), ("ring", 2, 1, 1, 1), ("ring", 1, 3, 1, 0), ("weigh", 1), ("ring", 1, 3, 1, 1),
+    ("weigh", 3), ("ring", 2, 2, 0, 0), ("ring", 2, 2, 0, 1), ("ring", 1, 4, 0, 0), ("ring", 2, 2, 1, 1),
+    ("ring", 2, 2, 1, 0), ("ring", 1, 4, 1, 1), ("mix", 2), ("weigh", 0), ("ring", 2, 3, 0, 0),
+    ("ring", 2, 3, 0, 1), ("ring", 2, 3, 1, 0), ("mix", 1), ("ring", 2, 3, 1, 1), ("mix", 3),
+    ("ring", 2, 4, 0, 0), ("ring", 2, 4, 1, 1), ("mix", 0),
+)
 
 
 def kernel(
@@ -104,8 +142,8 @@
     for t, (shard, whole) in enumerate(weights):
         keeps[t].start()
         send(shard, whole.at[1, me], start_recv.at[t, 1], me, far)
-    bias[:, 0:HB] = jnp.broadcast_to(b_text[...].astype(jnp.float32), (16, HB)).astype(jnp.bfloat16)
-    bias[:, HB : HB + KB] = jnp.broadcast_to(b_value[...].astype(jnp.float32), (16, KB)).astype(jnp.bfloat16)
+    bias[:, 0:HB] = jnp.broadcast_to(b_text[...].reshape(1, HB).astype(jnp.float32), (16, HB)).astype(jnp.bfloat16)
+    bias[:, HB : HB + KB] = jnp.broadcast_to(b_value[...].reshape(1, KB).astype(jnp.float32), (16, KB)).astype(jnp.bfloat16)
     send(bias, bias_far, bias_recv.at[0], me, far)
     fetch = [
         pltpu.make_async_copy(query.at[0, :, pl.ds(b * KB, KB)], qv.at[b], query_sem.at[b])
@@ -134,42 +172,36 @@
         give(t, h, a, 0, 0, -1, 5 + 4 * index)
         share(t, h, a, 0)
 
-    def flow_own(t, h):
+    PLACES = (0, -1, 1, 2)
+
+    def own(t, h):
         arrive(weights[t][1].at[h, me], start_recv.at[t, h])
         give(t, h, 0, 0, 1, 0, 0)
         give(t, h, 0, 0, -1, 0, 1)
         across(t, h, 0, 0)
 
-    def flow_near(t, h):
-        arrive(piece(t, h, -1, 0), flow_recv.at[t, h, 0])
-        give(t, h, -1, 0, 1, 0, 2, 0)
-        across(t, h, -1, 1)
-        arrive(piece(t, h, 1, 0), flow_recv.at[t, h, 1])
-        give(t, h, 1, 0, -1, 0, 3, 1)
-        across(t, h, 1, 2)
-
-    def flow_far(t, h):
+    def near(t, h, side):
+        index = PLACES.index(side)
+        arrive(piece(t, h, side, 0), flow_recv.at[t, h, index - 1])
+        give(t, h, side, 0, -side, 0, index + 1, index - 1)
+        across(t, h, side, index)
+
+    def far_off(t, h):
         arrive(piece(t, h, 2, 0, 0), flow_recv.at[t, h, 2])
         arrive(piece(t, h, 2, 0, 1), flow_recv.at[t, h, 3])
         across(t, h, 2, 3)
 
-    PLACES = (0, -1, 1, 2)
-
-    def flow_second(t, h, *indices):
-        for index in indices:
-            a = PLACES[index]
-            arrive(piece(t, h, a, -1), flow_recv.at[t, h, 4 + 4 * index])
-            give(t, h, a, -1, 0, 1, 6 + 4 * index, 0)
-            share(t, h, a, -1)
-            arrive(piece(t, h, a, 1), flow_recv.at[t, h, 5 + 4 * index])
-            give(t, h, a, 1, 0, -1, 7 + 4 * index, 1)
-            share(t, h, a, 1)
-
-    def flow_last(t, h):
-        for index, a in enumerate(PLACES):
-            arrive(piece(t, h, a, 2, 0), flow_recv.at[t, h, 6 + 4 * index])
-            arrive(piece(t, h, a, 2, 1), flow_recv.at[t, h, 7 + 4 * index])
-            share(t, h, a, 2)
+    def second(t, h, index, side):
+        a, part = PLACES[index], (1 + side) // 2
+        arrive(piece(t, h, a, side), flow_recv.at[t, h, 4 + 4 * index + part])
+        give(t, h, a, side, 0, -side, 6 + 4 * index + part, part)
+        share(t, h, a, side)
+
+    def last(t, h, index):
+        a = PLACES[index]
+        arrive(piece(t, h, a, 2, 0), flow_recv.at[t, h, 6 + 4 * index])
+        arrive(piece(t, h, a, 2, 1), flow_recv.at[t, h, 7 + 4 * index])
+        share(t, h, a, 2)
 
     def flow_twin(t, h):
         arrive(weights[t][1].at[h, 0 : NJ // 2], twin_recv.at[t, h])
@@ -226,29 +258,6 @@
         arrive(lines(p, -way, 1), text_recv.at[p, (1 - way) // 2])
         arrive(lines(p, way, 2), text_recv.at[p, 2])
 
-    flow_own(0, 0)
-    route_on(0)
-    flow_near(0, 0)
-    route_on(1)
-    flow_own(0, 1)
-    flow_far(0, 0)
-    flow_second(0, 0, 0)
-    text_on(0)
-    flow_second(0, 0, 1, 2)
-    flow_near(0, 1)
-    text_on(1)
-    text_pass(0)
-    flow_second(0, 0, 3)
-    flow_far(0, 1)
-    flow_second(0, 1, 0)
-    text_pass(1)
-    flow_last(0, 0)
-    flow_second(0, 1, 1, 2, 3)
-    flow_own(1, 0)
-    text_last(0)
-    text_last(1)
-    flow_twin(0, 0)
-
     def chunk(b, k):
         return hid.at[b, k * ROWS : (k + 1) * ROWS]
 
@@ -259,6 +268,12 @@
         arrive(chunk(b, k - way), hid_recv.at[h, 0 if way == 1 else 1, hop, k])
 
     def embed(h):
+        if h == 0:
+            text_last(0)
+            text_last(1)
+        else:
+            arrive(bias_far, bias_recv.at[0])
+        flow_twin(0, h)
         acc[...] = jnp.zeros_like(acc)
 
         @pl.loop(0, 4)
@@ -275,16 +290,16 @@
             hid_send(block(h), k, 1, 0, h)
             hid_send(block(h), 3 - k, -1, 0, h)
 
-    def hid_pass(h, hop):
-        for k in range(3, hop - 1, -1):
-            for way in (1, -1):
-                src = (k - hop + 1) if way == 1 else 3 - (k - hop + 1)
-                b = lax.rem(block(h) - way * hop + NZ, NZ)
-                hid_wait(b, src, way, hop - 1, h)
-                if k > hop:
-                    hid_send(b, src - way, way, hop, h)
-
-    def project(whole, h, target, with_bias):
+    def hidden(h, hop, k, way):
+        src = (k - hop + 1) if way == 1 else 3 - (k - hop + 1)
+        b = lax.rem(block(h) - way * hop + NZ, NZ)
+        hid_wait(b, src, way, hop - 1, h)
+        if k > hop:
+            hid_send(b, src - way, way, hop, h)
+
+    def project(t, h):
+        whole, target, sems = ((wk, kall, key_recv), (wv, vall, value_recv))[t - 1]
+        flow_twin(t, h)
         acc[:, 0:KB] = jnp.zeros((WIN, KB), jnp.float32)
 
         @pl.loop(0, NZ)
@@ -293,83 +308,22 @@
             acc[:, 0:KB] += jnp.dot(hid[b], part, preferred_element_type=jnp.float32)
 
         total = acc[:, 0:KB]
-        if with_bias:
+        if t == 2:
             total = total + (bias if h == 0 else bias_far)[0:1, HB : HB + KB].astype(jnp.float32)
         target[z, h] = total.astype(jnp.bfloat16)
-
-    def ring_send(target, sems, s, h):
         for way in (0, 1):
-            if s < (4 if way == h else 3):
-                origin = lax.rem(z + (NZ - s if way == 0 else s), NZ)
-                ref = target.at[origin, h]
-                send(ref, ref, sems.at[way, s, h], me, up if way == 0 else down)
-
-    def ring_wait(target, sems, s, h):
-        for way in (0, 1):
-            if s <= (4 if way == h else 3):
-                origin = lax.rem(z + (NZ - s if way == 0 else s), NZ)
-                arrive(target.at[origin, h], sems.at[way, s - 1, h])
-
-    def ring_step(target, sems, s):
-        for h in range(2):
-            ring_wait(target, sems, s, h)
-            if s < 4:
-                ring_send(target, sems, s, h)
-
-    embed(0)
-    flow_last(0, 1)
-    flow_near(1, 0)
-    hid_pass(0, 1)
-    flow_own(1, 1)
-    flow_far(1, 0)
-    flow_second(1, 0, 0)
-    arrive(bias_far, bias_recv.at[0])
-    flow_twin(0, 1)
-    embed(1)
-    hid_pass(0, 2)
-    flow_second(1, 0, 1, 2)
-    hid_pass(1, 1)
-    flow_near(1, 1)
-    hid_pass(0, 3)
-    flow_second(1, 0, 3)
-    hid_pass(1, 2)
-    flow_far(1, 1)
-    flow_second(1, 1, 0)
-    hid_pass(1, 3)
-    flow_last(1, 0)
-    flow_second(1, 1, 1, 2, 3)
-    flow_own(2, 0)
-    flow_twin(1, 0)
-    project(wk, 0, kall, False)
-    ring_send(kall, key_recv, 0, 0)
-    flow_last(1, 1)
-    flow_near(2, 0)
-    flow_own(2, 1)
-    flow_twin(1, 1)
-    project(wk, 1, kall, False)
-    ring_send(kall, key_recv, 0, 1)
-    flow_far(2, 0)
-    flow_second(2, 0, 0)
-    ring_step(kall, key_recv, 1)
-    flow_second(2, 0, 1, 2)
-    flow_near(2, 1)
-    ring_step(kall, key_recv, 2)
-    flow_second(2, 0, 3)
-    flow_far(2, 1)
-    flow_second(2, 1, 0)
-    ring_step(kall, key_recv, 3)
-    flow_last(2, 0)
-    flow_second(2, 1, 1, 2, 3)
-    flow_twin(2, 0)
-    project(wv, 0, vall, True)
-    ring_send(vall, value_recv, 0, 0)
-    flow_last(2, 1)
-    ring_step(kall, key_recv, 4)
-    flow_twin(2, 1)
-    project(wv, 1, vall, True)
-    ring_send(vall, value_recv, 0, 1)
-    for copy in fetch:
-        copy.wait()
+            ring_send(target, sems, 0, h, way)
+
+    def ring_send(target, sems, s, h, way):
+        if s < (4 if way == h else 3):
+            ref = target.at[lax.rem(z + (NZ - s if way == 0 else s), NZ), h]
+            send(ref, ref, sems.at[way, s, h], me, up if way == 0 else down)
+
+    def ring(t, s, h, way):
+        target, sems = ((kall, key_recv), (vall, value_recv))[t - 1]
+        origin = lax.rem(z + (NZ - s if way == 0 else s), NZ)
+        arrive(target.at[origin, h], sems.at[way, s - 1, h])
+        ring_send(target, sems, s, h, way)
 
     live = text_len[me]
     scale = HD ** (-0.5)
@@ -381,7 +335,8 @@
 
     NT = (((1,), (1,)), ((), ()))
 
-    def weigh(q):
+    def weigh(d):
+        q = lax.rem(z + d, 4)
         @pl.loop(0, 2)
         def _(n):
             b = lax.rem(q + 4 * n, NZ)
@@ -398,7 +353,8 @@
                 prob[b, i, :, 0:WIN] = (ea * share_of).astype(jnp.bfloat16)
                 prob[b, i, :, WIN:TXT] = (eb * share_of).astype(jnp.bfloat16)
 
-    def mix(q):
+    def mix(d):
+        q = lax.rem(z + d, 4)
         @pl.loop(0, 2)
         def _(n):
             b = lax.rem(q + 4 * n, NZ)
@@ -409,21 +365,16 @@
                 total += jnp.dot(prob[b, i, :, WIN:TXT], vall[other, 1, :, cols], preferred_element_type=jnp.float32)
                 out[0, :, pl.ds(pl.multiple_of(b * KB + i * HD, HD), HD)] = total.astype(jnp.bfloat16)
 
-    def quarter(d):
-        return lax.rem(z + d, 4)
-
-    weigh(quarter(2))
-    ring_step(vall, value_recv, 1)
-    weigh(quarter(1))
-    ring_step(vall, value_recv, 2)
-    weigh(quarter(3))
-    weigh(quarter(0))
-    ring_step(vall, value_recv, 3)
-    mix(quarter(2))
-    mix(quarter(1))
-    mix(quarter(3))
-    ring_step(vall, value_recv, 4)
-    mix(quarter(0))
+    acts = {
+        "own": own, "near": near, "far": far_off, "second": second, "last": last, "route_on": route_on,
+        "text_on": text_on, "text_pass": text_pass, "embed": embed, "hid": hidden, "project": project,
+        "ring": ring, "weigh": weigh, "mix": mix,
+    }
+    for name, *where in STEPS:
+        if name == "weigh" and where[0] == 2:
+            for copy in fetch:
+                copy.wait()
+        acts[name](*where)
 
     for copy in pending:
         copy.wait_send()
@@ -476,7 +427,7 @@
         compiler_params=pltpu.CompilerParams(
             collective_id=0, has_side_effects=True, vmem_limit_bytes=56 * 2**20
         ),
-    )(text_cache, source, text_len, query, w_text, w_key, w_value, b_text[None], b_value[None])
+    )(text_cache, source, text_len, query, w_text, w_key, w_value, b_text, b_value)
 
 
 def solution(mesh):

time: 169 us -> 160 us (0.947)
  Pallas kernels: 165 us -> 158 us
  local copies, waits for them, and re-layouts: 3.68 us -> 1.15 us
    pallas_call x1, Pallas kernels: 165 us -> 158 us  [body(): pl.pallas_call(kernel, out_shape=pltpu.VMEM((1, VR, HQ), bf16), in_specs=...]
    broadcast_in_dim x2 -> x0, local copies, waits for them, and re-layouts: 2.53 us -> none  [the longest x1 1.27 us: body(): b_value[None]]
where the time goes in v3:
time: 160 us; the launch traced here: 159 us
  Pallas kernels  158 us (99%)
    pallas_call x1, Pallas kernels, body(): pl.pallas_call(kernel, out_shape=pltpu.VMEM((1, VR, HQ), bf16), in_specs=...  158 us

profile of v3, /device:TPU:1, one launch (start us, length us, event | category | flops | bytes accessed | tf_op | source)
XLA Modules:
  0.0 159.4 jit_solution(1832765195552974897)
XLA Ops:
  0.0 158.3 %shard_map.91 = bf16[1,256,3072]{2,1,0:T(8,128)(2,1)S(1)} custom-call(bf16[1,2,64,4096]{3,2,1,0:T(8,128)(2,1)} %cache.1, s32[32]{0:T(128)} %source.1, s32[32]{0:T(128)} %text_len.1, bf16[1,256,3072]{2,1,0:T(8,128)(2,1)} %query.1, bf16[128,640]{1,0:T(8,128)(2,1)} %w_text.1, bf16[160,384]{1,0:T(8,128)(2,1)} %w_key.1, bf16[160,384]{1,0:T(8,128)(2,1)} %w_value.1, ...), custom_call_target="tpu_custom_call" | custom-call | tf_op jit(solution)/shard_map/pallas_call | solution.py:392
  158.3 1.1 copy.11

commit v4 on v3

--- a/solution.py
+++ b/solution.py
@@ -16,42 +16,49 @@
 WIN = 256
 DEPTHS = (DT // NJ, DM // NJ, DM // NJ)
 HALF = ROWS // 2
-N_SEND = 320
+N_SEND = 352
+SPOT = (2, 0, 1, 3)
 STEPS = (
     ("route_on", 0), ("own", 0, 0), ("route_on", 1), ("near", 0, 0, -1), ("near", 0, 0, 1), ("text_on", 0),
-    ("second", 0, 0, 0, -1), ("second", 0, 0, 0, 1), ("own", 0, 1), ("second", 0, 0, 1, 1), ("text_on", 1),
-    ("far", 0, 0), ("second", 0, 0, 1, -1), ("text_pass", 0), ("second", 0, 0, 2, 1), ("second", 0, 0, 2, -1),
-    ("last", 0, 0, 0), ("near", 0, 1, 1), ("near", 0, 1, -1), ("second", 0, 1, 0, 1), ("second", 0, 1, 0, -1),
-    ("text_pass", 1), ("second", 0, 0, 3, -1), ("second", 0, 0, 3, 1), ("last", 0, 0, 1), ("last", 0, 0, 2),
-    ("second", 0, 1, 2, -1), ("second", 0, 1, 2, 1), ("far", 0, 1), ("second", 0, 1, 1, 1),
-    ("second", 0, 1, 1, -1), ("last", 0, 1, 0), ("own", 1, 0), ("last", 0, 0, 3), ("last", 0, 1, 2),
-    ("own", 1, 1), ("embed", 0), ("second", 0, 1, 3, -1), ("second", 0, 1, 3, 1), ("last", 0, 1, 1),
-    ("near", 1, 0, -1), ("near", 1, 0, 1), ("second", 1, 0, 0, 1), ("second", 1, 0, 0, -1), ("near", 1, 1, 1),
-    ("near", 1, 1, -1), ("second", 1, 1, 0, 1), ("second", 1, 1, 0, -1), ("hid", 0, 1, 3, 1),
-    ("hid", 0, 1, 3, -1), ("last", 0, 1, 3), ("hid", 0, 1, 2, 1), ("hid", 0, 1, 2, -1),
-    ("second", 1, 0, 1, 1), ("far", 1, 0), ("second", 1, 0, 1, -1), ("embed", 1), ("hid", 0, 2, 3, 1),
-    ("hid", 0, 2, 3, -1), ("hid", 0, 1, 1, 1), ("hid", 0, 1, 1, -1), ("second", 1, 0, 2, -1),
-    ("second", 1, 0, 2, 1), ("last", 1, 0, 0), ("second", 1, 1, 2, -1), ("second", 1, 1, 2, 1), ("far", 1, 1),
-    ("hid", 0, 2, 2, 1), ("hid", 0, 2, 2, -1), ("second", 1, 1, 1, 1), ("second", 1, 1, 1, -1),
-    ("last", 1, 1, 0), ("hid", 1, 1, 3, 1), ("hid", 1, 1, 3, -1), ("own", 2, 0), ("second", 1, 0, 3, -1),
-    ("second", 1, 0, 3, 1), ("last", 1, 0, 1), ("last", 1, 0, 2), ("hid", 1, 1, 2, 1), ("hid", 1, 1, 2, -1),
-    ("last", 1, 1, 2), ("own", 2, 1), ("hid", 1, 1, 1, 1), ("hid", 1, 1, 1, -1), ("second", 1, 1, 3, -1),
-    ("second", 1, 1, 3, 1), ("last", 1, 1, 1), ("hid", 0, 3, 3, 1), ("hid", 0, 3, 3, -1), ("near", 2, 0, 1),
-    ("near", 2, 0, -1), ("second", 2, 0, 0, 1), ("second", 2, 0, 0, -1), ("hid", 1, 2, 3, 1),
-    ("hid", 1, 2, 3, -1), ("last", 1, 0, 3), ("hid", 1, 2, 2, 1), ("near", 2, 1, 1), ("hid", 1, 2, 2, -1),
-    ("near", 2, 1, -1), ("second", 2, 1, 0, 1), ("second", 2, 1, 0, -1), ("last", 1, 1, 3),
-    ("hid", 1, 3, 3, 1), ("hid", 1, 3, 3, -1), ("project", 1, 0), ("project", 1, 1), ("far", 2, 0),
-    ("second", 2, 0, 1, -1), ("second", 2, 0, 1, 1), ("second", 2, 0, 2, -1), ("second", 2, 0, 2, 1),
-    ("last", 2, 0, 0), ("second", 2, 1, 2, -1), ("second", 2, 1, 2, 1), ("far", 2, 1), ("second", 2, 1, 1, 1),
-    ("second", 2, 1, 1, -1), ("last", 2, 1, 0), ("ring", 1, 1, 0, 0), ("ring", 1, 1, 0, 1),
-    ("second", 2, 0, 3, 1), ("second", 2, 0, 3, -1), ("last", 2, 0, 1), ("last", 2, 0, 2), ("last", 2, 1, 2),
-    ("second", 2, 1, 3, 1), ("second", 2, 1, 3, -1), ("ring", 1, 1, 1, 0), ("ring", 1, 1, 1, 1),
-    ("last", 2, 1, 1), ("last", 2, 0, 3), ("last", 2, 1, 3), ("project", 2, 0), ("ring", 1, 2, 0, 0),
-    ("ring", 1, 2, 0, 1), ("project", 2, 1), ("ring", 1, 2, 1, 0), ("ring", 1, 2, 1, 1), ("weigh", 2),
-    ("ring", 2, 1, 0, 0), ("ring", 2, 1, 0, 1), ("ring", 1, 3, 0, 0), ("ring", 1, 3, 0, 1),
-    ("ring", 2, 1, 1, 0), ("ring", 2, 1, 1, 1), ("ring", 1, 3, 1, 0), ("weigh", 1), ("ring", 1, 3, 1, 1),
-    ("weigh", 3), ("ring", 2, 2, 0, 0), ("ring", 2, 2, 0, 1), ("ring", 1, 4, 0, 0), ("ring", 2, 2, 1, 1),
-    ("ring", 2, 2, 1, 0), ("ring", 1, 4, 1, 1), ("mix", 2), ("weigh", 0), ("ring", 2, 3, 0, 0),
+    ("second", 0, 0, 0, -1), ("second", 0, 0, 0, 1), ("text_pass", 0, 0), ("own", 0, 1), ("text_pass", 0, 1),
+    ("second", 0, 0, 1, 1), ("text_on", 1), ("far", 0, 0), ("second", 0, 0, 1, -1), ("second", 0, 0, 2, 1),
+    ("second", 0, 0, 2, -1), ("last", 0, 0, 0), ("text_pass", 1, 0), ("near", 0, 1, 1), ("near", 0, 1, -1),
+    ("second", 0, 1, 0, 1), ("second", 0, 1, 0, -1), ("text_pass", 1, 1), ("second", 0, 0, 3, -1),
+    ("second", 0, 0, 3, 1), ("last", 0, 0, 1), ("last", 0, 0, 2), ("second", 0, 1, 2, -1),
+    ("second", 0, 1, 2, 1), ("far", 0, 1), ("second", 0, 1, 1, 1), ("second", 0, 1, 1, -1), ("last", 0, 1, 0),
+    ("own", 1, 0), ("last", 0, 0, 3), ("last", 0, 1, 2), ("own", 1, 1), ("embed", 0), ("second", 0, 1, 3, -1),
+    ("second", 0, 1, 3, 1), ("last", 0, 1, 1), ("near", 1, 0, -1), ("near", 1, 0, 1), ("second", 1, 0, 0, 1),
+    ("second", 1, 0, 0, -1), ("near", 1, 1, 1), ("near", 1, 1, -1), ("second", 1, 1, 0, 1),
+    ("second", 1, 1, 0, -1), ("hid", 0, 1, 3, 1), ("hid", 0, 1, 3, -1), ("last", 0, 1, 3),
+    ("hid", 0, 1, 2, 1), ("hid", 0, 1, 2, -1), ("second", 1, 0, 1, 1), ("far", 1, 0), ("second", 1, 0, 1, -1),
+    ("embed", 1), ("hid", 0, 2, 3, 1), ("hid", 0, 2, 3, -1), ("hid", 0, 1, 1, 1), ("hid", 0, 1, 1, -1),
+    ("second", 1, 0, 2, -1), ("second", 1, 0, 2, 1), ("last", 1, 0, 0), ("second", 1, 1, 2, -1),
+    ("second", 1, 1, 2, 1), ("far", 1, 1), ("hid", 0, 2, 2, 1), ("hid", 0, 2, 2, -1), ("second", 1, 1, 1, 1),
+    ("second", 1, 1, 1, -1), ("last", 1, 1, 0), ("hid", 1, 1, 3, 1), ("hid", 1, 1, 3, -1), ("own", 2, 0),
+    ("second", 1, 0, 3, -1), ("second", 1, 0, 3, 1), ("last", 1, 0, 1), ("last", 1, 0, 2),
+    ("hid", 1, 1, 2, 1), ("hid", 1, 1, 2, -1), ("last", 1, 1, 2), ("own", 2, 1), ("hid", 1, 1, 1, 1),
+    ("hid", 1, 1, 1, -1), ("second", 1, 1, 3, -1), ("second", 1, 1, 3, 1), ("last", 1, 1, 1),
+    ("hid", 0, 3, 3, 1), ("hid", 0, 3, 3, -1), ("near", 2, 0, 1), ("near", 2, 0, -1), ("second", 2, 0, 0, 1),
+    ("second", 2, 0, 0, -1), ("hid", 1, 2, 3, 1), ("hid", 1, 2, 3, -1), ("last", 1, 0, 3),
+    ("hid", 1, 2, 2, 1), ("near", 2, 1, 1), ("hid", 1, 2, 2, -1), ("near", 2, 1, -1), ("project", 1, 0, 0),
+    ("hid", 1, 3, 3, 1), ("hid", 1, 3, 3, -1), ("project", 1, 0, 1), ("last", 1, 1, 3),
+    ("second", 2, 0, 2, -1), ("far", 2, 0), ("second", 2, 0, 2, 1), ("second", 2, 1, 0, -1),
+    ("second", 2, 1, 0, 1), ("second", 2, 0, 1, 1), ("second", 2, 0, 1, -1), ("last", 2, 0, 0),
+    ("project", 1, 1, 0), ("project", 1, 1, 1), ("ring", 1, 1, 0, 0, 0), ("ring", 1, 1, 0, 1, 0),
+    ("ring", 1, 1, 0, 0, 1), ("ring", 1, 1, 0, 1, 1), ("far", 2, 1), ("second", 2, 1, 1, -1),
+    ("second", 2, 1, 1, 1), ("second", 2, 1, 2, -1), ("second", 2, 1, 2, 1), ("second", 2, 0, 3, 1),
+    ("last", 2, 0, 2), ("second", 2, 0, 3, -1), ("ring", 1, 1, 1, 0, 0), ("ring", 1, 1, 1, 1, 0),
+    ("last", 2, 1, 0), ("last", 2, 0, 1), ("ring", 1, 1, 1, 0, 1), ("ring", 1, 1, 1, 1, 1),
+    ("second", 2, 1, 3, 1), ("second", 2, 1, 3, -1), ("last", 2, 1, 1), ("last", 2, 1, 2),
+    ("ring", 1, 2, 0, 0, 0), ("ring", 1, 2, 0, 1, 0), ("last", 2, 0, 3), ("last", 2, 1, 3),
+    ("ring", 1, 2, 0, 0, 1), ("ring", 1, 2, 0, 1, 1), ("project", 2, 0), ("ring", 1, 2, 1, 0, 0),
+    ("ring", 1, 2, 1, 1, 0), ("project", 2, 1), ("ring", 1, 2, 1, 0, 1), ("ring", 1, 2, 1, 1, 1),
+    ("weigh", 2), ("ring", 1, 3, 0, 0, 0), ("ring", 1, 3, 0, 1, 0), ("ring", 1, 3, 0, 0, 1),
+    ("ring", 1, 3, 0, 1, 1), ("ring", 2, 1, 0, 0), ("ring", 2, 1, 0, 1), ("ring", 1, 3, 1, 0, 0),
+    ("ring", 1, 3, 1, 1, 0), ("ring", 2, 1, 1, 0), ("ring", 2, 1, 1, 1), ("ring", 1, 3, 1, 0, 1),
+    ("weigh", 1), ("ring", 1, 3, 1, 1, 1), ("ring", 1, 4, 0, 0, 0), ("weigh", 3), ("ring", 2, 2, 0, 1),
+    ("ring", 1, 4, 0, 0, 1), ("ring", 1, 4, 1, 1, 0), ("ring", 2, 2, 0, 0), ("ring", 2, 2, 1, 1),
+    ("ring", 2, 2, 1, 0), ("ring", 1, 4, 1, 1, 1), ("mix", 2), ("weigh", 0), ("ring", 2, 3, 0, 0),
     ("ring", 2, 3, 0, 1), ("ring", 2, 3, 1, 0), ("mix", 1), ("ring", 2, 3, 1, 1), ("mix", 3),
     ("ring", 2, 4, 0, 0), ("ring", 2, 4, 1, 1), ("mix", 0),
 )
@@ -238,28 +245,34 @@
 
         own_job[p].start()
 
-    def lines(p, way, hops):
+    def lines(p, way, hops, side):
         at = first_row(p) - way * hops * ROWS
-        return txt.at[at : at + HALF]
+        return txt.at[at : at + HALF, side * (DT // 2) : (side + 1) * (DT // 2)]
+
+    def text_send(p, way, hops, side):
+        to, sem = up if way == 1 else down, text_recv.at[p, (1 + way) // 2 if hops == 0 else 2, side]
+        send(lines(p, way, hops, side), lines(p, way, hops + 1, side), sem, me, to)
 
     def text_on(p):
         own_job[p].wait()
         arrive(picked.at[p, pl.ds(0, NJ - 1)], route_recv.at[1, p])
         for way in (2 * p - 1, 1 - 2 * p):
-            send(lines(p, way, 0), lines(p, way, 1), text_recv.at[p, (1 + way) // 2], me, up if way == 1 else down)
-
-    def text_pass(p):
+            for side in range(2):
+                text_send(p, way, 0, side)
+
+    def text_pass(p, side):
         way = 2 * p - 1
-        arrive(lines(p, way, 1), text_recv.at[p, (1 + way) // 2])
-        send(lines(p, way, 1), lines(p, way, 2), text_recv.at[p, 2], me, up if way == 1 else down)
+        arrive(lines(p, way, 1, side), text_recv.at[p, (1 + way) // 2, side])
+        text_send(p, way, 1, side)
 
     def text_last(p):
         way = 2 * p - 1
-        arrive(lines(p, -way, 1), text_recv.at[p, (1 - way) // 2])
-        arrive(lines(p, way, 2), text_recv.at[p, 2])
+        for side in range(2):
+            arrive(lines(p, -way, 1, side), text_recv.at[p, (1 - way) // 2, side])
+            arrive(lines(p, way, 2, side), text_recv.at[p, 2, side])
 
     def chunk(b, k):
-        return hid.at[b, k * ROWS : (k + 1) * ROWS]
+        return hid.at[b, SPOT[k] * ROWS : (SPOT[k] + 1) * ROWS]
 
     def hid_send(b, k, way, hop, h):
         send(chunk(b, k), chunk(b, k - way), hid_recv.at[h, 0 if way == 1 else 1, hop, k], me, up if way == 1 else down)
@@ -285,7 +298,7 @@
         beside = (bias if h == 0 else bias_far)[0:1, 0:HB].astype(jnp.float32)
         for r in range(4):
             rows = slice(r * ROWS, (r + 1) * ROWS)
-            hid[block(h), rows, :] = jax.nn.gelu(acc[rows, :] + beside, approximate=True).astype(jnp.bfloat16)
+            chunk(block(h), r)[...] = jax.nn.gelu(acc[rows, :] + beside, approximate=True).astype(jnp.bfloat16)
         for k in (3, 2, 1):
             hid_send(block(h), k, 1, 0, h)
             hid_send(block(h), 3 - k, -1, 0, h)
@@ -297,39 +310,54 @@
         if k > hop:
             hid_send(b, src - way, way, hop, h)
 
-    def project(t, h):
-        whole, target, sems = ((wk, kall, key_recv), (wv, vall, value_recv))[t - 1]
-        flow_twin(t, h)
-        acc[:, 0:KB] = jnp.zeros((WIN, KB), jnp.float32)
+    def matmul(whole, h, rows):
+        acc[rows, 0:KB] = jnp.zeros((rows.stop - rows.start, KB), jnp.float32)
 
         @pl.loop(0, NZ)
         def _(b):
             part = whole[h, pl.ds(b * 4, 4)].reshape(HB, KB)
-            acc[:, 0:KB] += jnp.dot(hid[b], part, preferred_element_type=jnp.float32)
-
-        total = acc[:, 0:KB]
-        if t == 2:
+            acc[rows, 0:KB] += jnp.dot(hid[b, rows, :], part, preferred_element_type=jnp.float32)
+
+        return acc[rows, 0:KB]
+
+    def half(part):
+        return slice(part * (WIN // 2), (part + 1) * (WIN // 2))
+
+    def project(t, h, part=None):
+        if not part:
+            flow_twin(t, h)
+        if t == 1:
+            kall[z, h, half(part), :] = matmul(wk, h, half(part)).astype(jnp.bfloat16)
+        else:
+            total = matmul(wv, h, slice(0, WIN))
             total = total + (bias if h == 0 else bias_far)[0:1, HB : HB + KB].astype(jnp.float32)
-        target[z, h] = total.astype(jnp.bfloat16)
+            vall[z, h] = total.astype(jnp.bfloat16)
         for way in (0, 1):
-            ring_send(target, sems, 0, h, way)
-
-    def ring_send(target, sems, s, h, way):
+            ring_send(t, 0, h, way, part)
+
+    def ring_piece(t, s, h, way, part):
+        origin = lax.rem(z + (NZ - s if way == 0 else s), NZ)
+        return kall.at[origin, h, half(part)] if t == 1 else vall.at[origin, h]
+
+    def ring_sem(t, s, h, way, part):
+        return key_recv.at[way, s, h, part] if t == 1 else value_recv.at[way, s, h]
+
+    def ring_send(t, s, h, way, part):
         if s < (4 if way == h else 3):
-            ref = target.at[lax.rem(z + (NZ - s if way == 0 else s), NZ), h]
-            send(ref, ref, sems.at[way, s, h], me, up if way == 0 else down)
-
-    def ring(t, s, h, way):
-        target, sems = ((kall, key_recv), (vall, value_recv))[t - 1]
-        origin = lax.rem(z + (NZ - s if way == 0 else s), NZ)
-        arrive(target.at[origin, h], sems.at[way, s - 1, h])
-        ring_send(target, sems, s, h, way)
+            ref = ring_piece(t, s, h, way, part)
+            send(ref, ref, ring_sem(t, s, h, way, part), me, up if way == 0 else down)
+
+    def ring(t, s, h, way, part=None):
+        arrive(ring_piece(t, s, h, way, part), ring_sem(t, s - 1, h, way, part))
+        ring_send(t, s, h, way, part)
 
     live = text_len[me]
     scale = HD ** (-0.5)
 
     def dead(origin):
-        at = lax.broadcasted_iota(jnp.int32, (1, WIN), 1) + (ROWS * origin - 96)
+        at = lax.broadcasted_iota(jnp.int32, (1, WIN), 1)
+        at = jnp.where(at < 2 * ROWS, at + ROWS, jnp.where(at < 3 * ROWS, at - 2 * ROWS, at))
+        at = at + (ROWS * origin - 96)
         at = jnp.where(at < 0, at + TXT, jnp.where(at >= TXT, at - TXT, at))
         return jnp.where(at < live, jnp.float32(0), jnp.float32(-1e30))
 
@@ -365,6 +393,16 @@
                 total += jnp.dot(prob[b, i, :, WIN:TXT], vall[other, 1, :, cols], preferred_element_type=jnp.float32)
                 out[0, :, pl.ds(pl.multiple_of(b * KB + i * HD, HD), HD)] = total.astype(jnp.bfloat16)
 
+    def drain(count):
+        for copy in pending[:count]:
+            copy.wait_send()
+        for p in range(2):
+
+            @pl.loop(1, NJ)
+            def _(i):
+                slab_copy(p, i).wait_send()
+                job_copy(p, i).wait_send()
+
     acts = {
         "own": own, "near": near, "far": far_off, "second": second, "last": last, "route_on": route_on,
         "text_on": text_on, "text_pass": text_pass, "embed": embed, "hid": hidden, "project": project,
@@ -374,16 +412,16 @@
         if name == "weigh" and where[0] == 2:
             for copy in fetch:
                 copy.wait()
+        if (name, *where) == ("ring", 2, 4, 0, 0):
+            drain(early)
+            drained = early
         acts[name](*where)
-
-    for copy in pending:
+        if (name, *where) == ("project", 2, 1):
+            early = len(pending)
+
+
+    for copy in pending[drained:]:
         copy.wait_send()
-    for p in range(2):
-
-        @pl.loop(1, NJ)
-        def _(i):
-            slab_copy(p, i).wait_send()
-            job_copy(p, i).wait_send()
 
 
 def body(text_cache, source, text_len, query, w_text, b_text, w_key, w_value, b_value):
@@ -417,9 +455,9 @@
             dma((3, 2)),
             dma((3, 2, 20)),
             dma((3, 2)),
-            dma((2, 3)),
+            dma((2, 3, 2)),
             dma((2, 2, 3, 4)),
-            dma((2, 4, 2)),
+            dma((2, 4, 2, 2)),
             dma((2, 4, 2)),
             dma((1,)),
             dma((NZ,)),

time: 160 us -> 157 us (0.981)
  Pallas kernels: 158 us -> 156 us
    pallas_call x1, Pallas kernels: 158 us -> 156 us  [body(): pl.pallas_call(kernel, out_shape=pltpu.VMEM((1, VR, HQ), bf16), in_specs=...]
where the time goes in v4:
time: 157 us
  Pallas kernels  156 us (99%)
    pallas_call x1, Pallas kernels, body(): pl.pallas_call(kernel, out_shape=pltpu.VMEM((1, VR, HQ), bf16), in_specs=...  156 us

profile of v4, /device:TPU:1, one launch (start us, length us, event | category | flops | bytes accessed | tf_op | source)
XLA Modules:
  0.0 157.1 jit_solution(8978684730533371700)
XLA Ops:
  0.0 155.9 %shard_map.91 = bf16[1,256,3072]{2,1,0:T(8,128)(2,1)S(1)} custom-call(bf16[1,2,64,4096]{3,2,1,0:T(8,128)(2,1)} %cache.1, s32[32]{0:T(128)} %source.1, s32[32]{0:T(128)} %text_len.1, bf16[1,256,3072]{2,1,0:T(8,128)(2,1)} %query.1, bf16[128,640]{1,0:T(8,128)(2,1)} %w_text.1, bf16[160,384]{1,0:T(8,128)(2,1)} %w_key.1, bf16[160,384]{1,0:T(8,128)(2,1)} %w_value.1, ...), custom_call_target="tpu_custom_call" | custom-call | tf_op jit(solution)/shard_map/pallas_call | solution.py:430
  155.9 1.1 copy.11

commit v5 on v4

--- a/solution.py
+++ b/solution.py
@@ -19,48 +19,48 @@
 N_SEND = 352
 SPOT = (2, 0, 1, 3)
 STEPS = (
-    ("route_on", 0), ("own", 0, 0), ("route_on", 1), ("near", 0, 0, -1), ("near", 0, 0, 1), ("text_on", 0),
-    ("second", 0, 0, 0, -1), ("second", 0, 0, 0, 1), ("text_pass", 0, 0), ("own", 0, 1), ("text_pass", 0, 1),
-    ("second", 0, 0, 1, 1), ("text_on", 1), ("far", 0, 0), ("second", 0, 0, 1, -1), ("second", 0, 0, 2, 1),
-    ("second", 0, 0, 2, -1), ("last", 0, 0, 0), ("text_pass", 1, 0), ("near", 0, 1, 1), ("near", 0, 1, -1),
-    ("second", 0, 1, 0, 1), ("second", 0, 1, 0, -1), ("text_pass", 1, 1), ("second", 0, 0, 3, -1),
-    ("second", 0, 0, 3, 1), ("last", 0, 0, 1), ("last", 0, 0, 2), ("second", 0, 1, 2, -1),
-    ("second", 0, 1, 2, 1), ("far", 0, 1), ("second", 0, 1, 1, 1), ("second", 0, 1, 1, -1), ("last", 0, 1, 0),
-    ("own", 1, 0), ("last", 0, 0, 3), ("last", 0, 1, 2), ("own", 1, 1), ("embed", 0), ("second", 0, 1, 3, -1),
-    ("second", 0, 1, 3, 1), ("last", 0, 1, 1), ("near", 1, 0, -1), ("near", 1, 0, 1), ("second", 1, 0, 0, 1),
-    ("second", 1, 0, 0, -1), ("near", 1, 1, 1), ("near", 1, 1, -1), ("second", 1, 1, 0, 1),
-    ("second", 1, 1, 0, -1), ("hid", 0, 1, 3, 1), ("hid", 0, 1, 3, -1), ("last", 0, 1, 3),
-    ("hid", 0, 1, 2, 1), ("hid", 0, 1, 2, -1), ("second", 1, 0, 1, 1), ("far", 1, 0), ("second", 1, 0, 1, -1),
-    ("embed", 1), ("hid", 0, 2, 3, 1), ("hid", 0, 2, 3, -1), ("hid", 0, 1, 1, 1), ("hid", 0, 1, 1, -1),
-    ("second", 1, 0, 2, -1), ("second", 1, 0, 2, 1), ("last", 1, 0, 0), ("second", 1, 1, 2, -1),
-    ("second", 1, 1, 2, 1), ("far", 1, 1), ("hid", 0, 2, 2, 1), ("hid", 0, 2, 2, -1), ("second", 1, 1, 1, 1),
-    ("second", 1, 1, 1, -1), ("last", 1, 1, 0), ("hid", 1, 1, 3, 1), ("hid", 1, 1, 3, -1), ("own", 2, 0),
-    ("second", 1, 0, 3, -1), ("second", 1, 0, 3, 1), ("last", 1, 0, 1), ("last", 1, 0, 2),
-    ("hid", 1, 1, 2, 1), ("hid", 1, 1, 2, -1), ("last", 1, 1, 2), ("own", 2, 1), ("hid", 1, 1, 1, 1),
-    ("hid", 1, 1, 1, -1), ("second", 1, 1, 3, -1), ("second", 1, 1, 3, 1), ("last", 1, 1, 1),
-    ("hid", 0, 3, 3, 1), ("hid", 0, 3, 3, -1), ("near", 2, 0, 1), ("near", 2, 0, -1), ("second", 2, 0, 0, 1),
-    ("second", 2, 0, 0, -1), ("hid", 1, 2, 3, 1), ("hid", 1, 2, 3, -1), ("last", 1, 0, 3),
-    ("hid", 1, 2, 2, 1), ("near", 2, 1, 1), ("hid", 1, 2, 2, -1), ("near", 2, 1, -1), ("project", 1, 0, 0),
-    ("hid", 1, 3, 3, 1), ("hid", 1, 3, 3, -1), ("project", 1, 0, 1), ("last", 1, 1, 3),
-    ("second", 2, 0, 2, -1), ("far", 2, 0), ("second", 2, 0, 2, 1), ("second", 2, 1, 0, -1),
-    ("second", 2, 1, 0, 1), ("second", 2, 0, 1, 1), ("second", 2, 0, 1, -1), ("last", 2, 0, 0),
-    ("project", 1, 1, 0), ("project", 1, 1, 1), ("ring", 1, 1, 0, 0, 0), ("ring", 1, 1, 0, 1, 0),
-    ("ring", 1, 1, 0, 0, 1), ("ring", 1, 1, 0, 1, 1), ("far", 2, 1), ("second", 2, 1, 1, -1),
-    ("second", 2, 1, 1, 1), ("second", 2, 1, 2, -1), ("second", 2, 1, 2, 1), ("second", 2, 0, 3, 1),
-    ("last", 2, 0, 2), ("second", 2, 0, 3, -1), ("ring", 1, 1, 1, 0, 0), ("ring", 1, 1, 1, 1, 0),
-    ("last", 2, 1, 0), ("last", 2, 0, 1), ("ring", 1, 1, 1, 0, 1), ("ring", 1, 1, 1, 1, 1),
-    ("second", 2, 1, 3, 1), ("second", 2, 1, 3, -1), ("last", 2, 1, 1), ("last", 2, 1, 2),
-    ("ring", 1, 2, 0, 0, 0), ("ring", 1, 2, 0, 1, 0), ("last", 2, 0, 3), ("last", 2, 1, 3),
-    ("ring", 1, 2, 0, 0, 1), ("ring", 1, 2, 0, 1, 1), ("project", 2, 0), ("ring", 1, 2, 1, 0, 0),
-    ("ring", 1, 2, 1, 1, 0), ("project", 2, 1), ("ring", 1, 2, 1, 0, 1), ("ring", 1, 2, 1, 1, 1),
-    ("weigh", 2), ("ring", 1, 3, 0, 0, 0), ("ring", 1, 3, 0, 1, 0), ("ring", 1, 3, 0, 0, 1),
-    ("ring", 1, 3, 0, 1, 1), ("ring", 2, 1, 0, 0), ("ring", 2, 1, 0, 1), ("ring", 1, 3, 1, 0, 0),
-    ("ring", 1, 3, 1, 1, 0), ("ring", 2, 1, 1, 0), ("ring", 2, 1, 1, 1), ("ring", 1, 3, 1, 0, 1),
-    ("weigh", 1), ("ring", 1, 3, 1, 1, 1), ("ring", 1, 4, 0, 0, 0), ("weigh", 3), ("ring", 2, 2, 0, 1),
-    ("ring", 1, 4, 0, 0, 1), ("ring", 1, 4, 1, 1, 0), ("ring", 2, 2, 0, 0), ("ring", 2, 2, 1, 1),
-    ("ring", 2, 2, 1, 0), ("ring", 1, 4, 1, 1, 1), ("mix", 2), ("weigh", 0), ("ring", 2, 3, 0, 0),
-    ("ring", 2, 3, 0, 1), ("ring", 2, 3, 1, 0), ("mix", 1), ("ring", 2, 3, 1, 1), ("mix", 3),
-    ("ring", 2, 4, 0, 0), ("ring", 2, 4, 1, 1), ("mix", 0),
+    ("own", 0, 0), ("route_on", 0), ("near", 0, 0, -1), ("near", 0, 0, 1), ("route_on", 1),
+    ("second", 0, 0, 0, -1), ("second", 0, 0, 0, 1), ("second", 0, 0, 1, 1), ("text_on", 0),
+    ("second", 0, 0, 1, -1), ("far", 0, 0), ("own", 0, 1), ("second", 0, 0, 2, -1), ("second", 0, 0, 2, 1),
+    ("text_pass", 0, 0), ("text_pass", 0, 1), ("last", 0, 0, 0), ("last", 0, 0, 1), ("text_on", 1),
+    ("second", 0, 0, 3, -1), ("second", 0, 0, 3, 1), ("near", 0, 1, -1), ("near", 0, 1, 1),
+    ("text_pass", 1, 0), ("second", 0, 1, 0, -1), ("second", 0, 1, 0, 1), ("last", 0, 0, 2),
+    ("last", 0, 0, 3), ("text_pass", 1, 1), ("second", 0, 1, 1, 1), ("second", 0, 1, 1, -1), ("far", 0, 1),
+    ("own", 1, 0), ("second", 0, 1, 2, -1), ("second", 0, 1, 2, 1), ("last", 0, 1, 0), ("last", 0, 1, 1),
+    ("embed", 0), ("second", 0, 1, 3, -1), ("second", 0, 1, 3, 1), ("near", 1, 0, -1), ("near", 1, 0, 1),
+    ("second", 1, 0, 0, -1), ("second", 1, 0, 0, 1), ("last", 0, 1, 2), ("last", 0, 1, 3), ("own", 1, 1),
+    ("hid", 0, 1, 3, 1), ("hid", 0, 1, 3, -1), ("second", 1, 0, 1, 1), ("second", 1, 0, 1, -1), ("far", 1, 0),
+    ("hid", 0, 1, 2, 1), ("hid", 0, 1, 2, -1), ("embed", 1), ("hid", 0, 1, 1, 1), ("hid", 0, 1, 1, -1),
+    ("second", 1, 0, 2, -1), ("second", 1, 0, 2, 1), ("last", 1, 0, 0), ("near", 1, 1, -1),
+    ("hid", 0, 2, 3, 1), ("hid", 0, 2, 3, -1), ("near", 1, 1, 1), ("second", 1, 1, 0, -1),
+    ("second", 1, 1, 0, 1), ("last", 1, 0, 1), ("hid", 0, 2, 2, 1), ("hid", 0, 2, 2, -1),
+    ("second", 1, 0, 3, -1), ("second", 1, 0, 3, 1), ("last", 1, 0, 2), ("hid", 1, 1, 3, 1),
+    ("hid", 1, 1, 3, -1), ("own", 2, 0), ("second", 1, 1, 1, 1), ("hid", 1, 1, 2, 1), ("hid", 1, 1, 2, -1),
+    ("second", 1, 1, 1, -1), ("far", 1, 1), ("second", 1, 1, 2, -1), ("second", 1, 1, 2, 1),
+    ("hid", 1, 1, 1, 1), ("hid", 1, 1, 1, -1), ("last", 1, 1, 0), ("last", 1, 0, 3), ("hid", 0, 3, 3, 1),
+    ("hid", 0, 3, 3, -1), ("near", 2, 0, -1), ("near", 2, 0, 1), ("hid", 1, 2, 3, 1), ("hid", 1, 2, 3, -1),
+    ("second", 2, 0, 0, -1), ("second", 2, 0, 0, 1), ("last", 1, 1, 1), ("hid", 1, 2, 2, 1),
+    ("hid", 1, 2, 2, -1), ("project", 1, 0, 0), ("last", 1, 1, 2), ("second", 1, 1, 3, -1),
+    ("second", 1, 1, 3, 1), ("hid", 1, 3, 3, 1), ("hid", 1, 3, 3, -1), ("project", 1, 0, 1), ("far", 2, 0),
+    ("second", 2, 0, 1, -1), ("second", 2, 0, 1, 1), ("own", 2, 1), ("second", 2, 0, 2, -1),
+    ("second", 2, 0, 2, 1), ("last", 2, 0, 0), ("ring", 1, 1, 0, 0, 0), ("ring", 1, 1, 0, 1, 0),
+    ("last", 1, 1, 3), ("second", 2, 0, 3, -1), ("second", 2, 0, 3, 1), ("ring", 1, 1, 0, 0, 1),
+    ("ring", 1, 1, 0, 1, 1), ("last", 2, 0, 1), ("project", 1, 1, 0), ("project", 1, 1, 1),
+    ("ring", 1, 2, 0, 0, 0), ("ring", 1, 2, 0, 1, 0), ("second", 2, 1, 0, -1), ("last", 2, 0, 2),
+    ("second", 2, 1, 0, 1), ("near", 2, 1, -1), ("near", 2, 1, 1), ("last", 2, 0, 3), ("ring", 1, 2, 0, 0, 1),
+    ("ring", 1, 2, 0, 1, 1), ("last", 2, 1, 0), ("ring", 1, 1, 1, 0, 0), ("ring", 1, 1, 1, 1, 0),
+    ("project", 2, 0), ("ring", 1, 1, 1, 0, 1), ("ring", 1, 1, 1, 1, 1), ("second", 2, 1, 1, -1),
+    ("second", 2, 1, 1, 1), ("second", 2, 1, 2, -1), ("second", 2, 1, 2, 1), ("far", 2, 1),
+    ("ring", 1, 3, 0, 0, 0), ("ring", 1, 3, 0, 1, 0), ("last", 2, 1, 1), ("ring", 1, 3, 0, 0, 1),
+    ("ring", 1, 3, 0, 1, 1), ("last", 2, 1, 2), ("second", 2, 1, 3, -1), ("second", 2, 1, 3, 1),
+    ("ring", 1, 2, 1, 0, 0), ("ring", 1, 2, 1, 1, 0), ("last", 2, 1, 3), ("ring", 2, 1, 0, 0),
+    ("ring", 2, 1, 0, 1), ("project", 2, 1), ("ring", 1, 2, 1, 0, 1), ("ring", 1, 2, 1, 1, 1), ("weigh", 2),
+    ("ring", 1, 3, 1, 1, 0), ("ring", 1, 4, 0, 0, 0), ("ring", 1, 4, 0, 0, 1), ("ring", 1, 3, 1, 0, 0),
+    ("ring", 2, 2, 0, 1), ("ring", 2, 2, 0, 0), ("ring", 2, 1, 1, 1), ("ring", 1, 3, 1, 1, 1), ("weigh", 3),
+    ("ring", 2, 1, 1, 0), ("ring", 1, 4, 1, 1, 0), ("ring", 1, 3, 1, 0, 1), ("weigh", 1),
+    ("ring", 2, 3, 0, 1), ("ring", 2, 3, 0, 0), ("ring", 2, 2, 1, 1), ("ring", 2, 2, 1, 0),
+    ("ring", 1, 4, 1, 1, 1), ("mix", 2), ("weigh", 0), ("ring", 2, 4, 0, 0), ("ring", 2, 3, 1, 1), ("mix", 3),
+    ("ring", 2, 3, 1, 0), ("mix", 1), ("ring", 2, 4, 1, 1), ("mix", 0),
 )
 
 

time: 157 us -> 154 us (0.981)
  Pallas kernels: 156 us -> 152 us
    pallas_call x1, Pallas kernels: 156 us -> 152 us  [body(): pl.pallas_call(kernel, out_shape=pltpu.VMEM((1, VR, HQ), bf16), in_specs=...]
where the time goes in v5:
time: 154 us
  Pallas kernels  152 us (99%)
    pallas_call x1, Pallas kernels, body(): pl.pallas_call(kernel, out_shape=pltpu.VMEM((1, VR, HQ), bf16), in_specs=...  152 us

profile of v5, /device:TPU:1, one launch (start us, length us, event | category | flops | bytes accessed | tf_op | source)
XLA Modules:
  0.0 153.5 jit_solution(3878977369957436091)
XLA Ops:
  0.0 152.4 %shard_map.91 = bf16[1,256,3072]{2,1,0:T(8,128)(2,1)S(1)} custom-call(bf16[1,2,64,4096]{3,2,1,0:T(8,128)(2,1)} %cache.1, s32[32]{0:T(128)} %source.1, s32[32]{0:T(128)} %text_len.1, bf16[1,256,3072]{2,1,0:T(8,128)(2,1)} %query.1, bf16[128,640]{1,0:T(8,128)(2,1)} %w_text.1, bf16[160,384]{1,0:T(8,128)(2,1)} %w_key.1, bf16[160,384]{1,0:T(8,128)(2,1)} %w_value.1, ...), custom_call_target="tpu_custom_call" | custom-call | tf_op jit(solution)/shard_map/pallas_call | solution.py:430
  152.4 1.1 copy.11

commit v6 on v5

--- a/solution.py
+++ b/solution.py
@@ -289,10 +289,10 @@
         flow_twin(0, h)
         acc[...] = jnp.zeros_like(acc)
 
-        @pl.loop(0, 4)
+        @pl.loop(0, 2)
         def _(i):
-            at = pl.ds(pl.multiple_of(i * 1024, 1024), 1024)
-            part = wt[h, pl.ds(i * 8, 8)].reshape(1024, HB)
+            at = pl.ds(pl.multiple_of(i * 2048, 2048), 2048)
+            part = wt[h, pl.ds(i * 16, 16)].reshape(2048, HB)
             acc[...] += jnp.dot(txt[:, at], part, preferred_element_type=jnp.float32)
 
         beside = (bias if h == 0 else bias_far)[0:1, 0:HB].astype(jnp.float32)
@@ -313,10 +313,11 @@
     def matmul(whole, h, rows):
         acc[rows, 0:KB] = jnp.zeros((rows.stop - rows.start, KB), jnp.float32)
 
-        @pl.loop(0, NZ)
+        @pl.loop(0, NZ // 2)
         def _(b):
-            part = whole[h, pl.ds(b * 4, 4)].reshape(HB, KB)
-            acc[rows, 0:KB] += jnp.dot(hid[b, rows, :], part, preferred_element_type=jnp.float32)
+            part = whole[h, pl.ds(b * 8, 8)].reshape(2 * HB, KB)
+            pair = jnp.concatenate([hid[2 * b, rows, :], hid[2 * b + 1, rows, :]], axis=1)
+            acc[rows, 0:KB] += jnp.dot(pair, part, preferred_element_type=jnp.float32)
 
         return acc[rows, 0:KB]
 

time: 154 us -> 153 us (level)
  Pallas kernels: 152 us -> 150 us
    pallas_call x1, Pallas kernels: 152 us -> 150 us  [body(): pl.pallas_call(kernel, out_shape=pltpu.VMEM((1, VR, HQ), bf16), in_specs=...]
where the time goes in v6:
time: 153 us; the launch traced here: 152 us
  Pallas kernels  150 us (98%)
    pallas_call x1, Pallas kernels, body(): pl.pallas_call(kernel, out_shape=pltpu.VMEM((1, VR, HQ), bf16), in_specs=...  150 us

profile of v6, /device:TPU:1, one launch (start us, length us, event | category | flops | bytes accessed | tf_op | source)
XLA Modules:
  0.0 151.5 jit_solution(4331057904676434873)
XLA Ops:
  0.0 150.4 %shard_map.91 = bf16[1,256,3072]{2,1,0:T(8,128)(2,1)S(1)} custom-call(bf16[1,2,64,4096]{3,2,1,0:T(8,128)(2,1)} %cache.1, s32[32]{0:T(128)} %source.1, s32[32]{0:T(128)} %text_len.1, bf16[1,256,3072]{2,1,0:T(8,128)(2,1)} %query.1, bf16[128,640]{1,0:T(8,128)(2,1)} %w_text.1, bf16[160,384]{1,0:T(8,128)(2,1)} %w_key.1, bf16[160,384]{1,0:T(8,128)(2,1)} %w_value.1, ...), custom_call_target="tpu_custom_call" | custom-call | tf_op jit(solution)/shard_map/pallas_call | solution.py:431
  150.4 1.1 copy.11
